TPU v7x, 128 devices: a whole 4x4x4 slice. The times are simulated.
128 devices in a mesh: ctx: 32 (over y, x, core), shard: 4 (over z).
Axes of the slice: x: 4, y: 4, z: 4, core: 2. Of those that a mesh axis runs over, the one named last changes fastest.
Arguments:
- hidden: bfloat16 [16384, 768], P(('shard', 'ctx')), may hold values from -6 to 6
- ln1_gain: bfloat16 [768], P('shard'), may hold values from 0.5 to 1.5
- ln1_bias: bfloat16 [768], P('shard'), may hold values from -1 to 1
- ln2_gain: bfloat16 [768], P('shard'), may hold values from 0.5 to 1.5
- ln2_bias: bfloat16 [768], P('shard'), may hold values from -1 to 1
- w_qkv: bfloat16 [768, 2304], P('shard'), may hold values from -0.21875 to 0.21875
- b_qkv: bfloat16 [2304], P('shard'), may hold values from -1 to 1
- w_out: bfloat16 [768, 768], P('shard'), may hold values from -1.75 to 1.75
- b_out: bfloat16 [768], P('shard'), may hold values from -1 to 1
- w_up: bfloat16 [768, 3072], P('shard'), may hold values from -0.21875 to 0.21875
- b_up: bfloat16 [3072], P('shard'), may hold values from -1 to 1
- w_down: bfloat16 [3072, 768], P('shard'), may hold values from -0.109375 to 0.109375
- b_down: bfloat16 [768], P('shard'), may hold values from -1 to 1
- block_order: int32 [4, 64], P('shard'), may hold values from 0 to 63, as said below
- positions: int32 [4, 4096], P('shard'), may hold values from 0 to 3071, as said below
- cotangent: bfloat16 [16384, 768], P(('shard', 'ctx')), may hold values from -6 to 6
Outputs:
- output: bfloat16 [16384, 768], P(('shard', 'ctx'))
- grad_input: float32 [16384, 768], P(('shard', 'ctx'))
- grad_ln1_gain: float32 [768], P('shard')
- grad_ln1_bias: float32 [768], P('shard')
- grad_ln2_gain: float32 [768], P('shard')
- grad_ln2_bias: float32 [768], P('shard')
- grad_w_qkv: float32 [768, 2304], P('shard')
- grad_b_qkv: float32 [2304], P('shard')
- grad_w_out: float32 [768, 768], P('shard')
- grad_b_out: float32 [768], P('shard')
- grad_w_up: float32 [768, 3072], P('shard')
- grad_b_up: float32 [3072], P('shard')
- grad_w_down: float32 [3072, 768], P('shard')
- grad_b_down: float32 [768], P('shard')
Inputs may be any that keep to these rules, and one draw needn't show every extreme that they name: Each row of block_order holds every number of 0 .. 63 once, and block_order[s, 2 c] + block_order[s, 2 c + 1] = 63 for every c. positions[s, t] is 0 at the first token of a document and rises by one from token to token within it; documents cover each sequence end to end.
All inputs are finite; a program needn't handle non-finite values.
Results may differ from a plain program's by a relative error of at most 0.03.
Values may be sent and summed in bfloat16 or wider, within the bound.
A program may use at most 192 MiB of HBM per device.

v0:
```python
import math

import jax
import jax.numpy as jnp
from jax import lax
from jax.sharding import PartitionSpec as P

HD = 64
ROT = 16


def layer_norm(values, gain, bias):
    center = values - jnp.mean(values, axis=-1, keepdims=True)
    variance = jnp.mean(center * center, axis=-1, keepdims=True)
    return center * lax.rsqrt(variance + 1e-05) * gain + bias


def rotate(values, cosine, sine):
    count = values.shape[0]
    heads = values.reshape(count, -1, HD)
    half = ROT // 2
    first = heads[..., :half]
    second = heads[..., half:ROT]
    cos_b = cosine[:, None, :]
    sin_b = sine[:, None, :]
    turned = jnp.concatenate(
        [first * cos_b - second * sin_b, second * cos_b + first * sin_b, heads[..., ROT:]], axis=-1
    )
    return turned.reshape(count, -1)


def tables(places):
    freqs = jnp.power(10000.0, -jnp.arange(0, ROT, 2, dtype=jnp.float32) / ROT)
    angle = places.astype(jnp.float32)[:, None] * freqs[None, :]
    return (jnp.cos(angle), jnp.sin(angle))


def exact_gelu(values):
    return jax.nn.gelu(values, approximate=False)


def local(
    hidden,
    ln1_gain,
    ln1_bias,
    ln2_gain,
    ln2_bias,
    w_qkv,
    b_qkv,
    w_out,
    b_out,
    w_up,
    b_up,
    w_down,
    b_down,
    block_order,
    positions,
    cotangent,
):
    params = (
        ln1_gain,
        ln1_bias,
        ln2_gain,
        ln2_bias,
        w_qkv,
        b_qkv,
        w_out,
        b_out,
        w_up,
        b_up,
        w_down,
        b_down,
    )
    gathered = (
        lax.all_gather(params[0], "shard", axis=0, tiled=True),
        lax.all_gather(params[1], "shard", axis=0, tiled=True),
        lax.all_gather(params[2], "shard", axis=0, tiled=True),
        lax.all_gather(params[3], "shard", axis=0, tiled=True),
        lax.all_gather(params[4], "shard", axis=0, tiled=True),
        lax.all_gather(params[5], "shard", axis=0, tiled=True),
        lax.all_gather(params[6], "shard", axis=0, tiled=True),
        lax.all_gather(params[7], "shard", axis=0, tiled=True),
        lax.all_gather(params[8], "shard", axis=0, tiled=True),
        lax.all_gather(params[9], "shard", axis=0, tiled=True),
        lax.all_gather(params[10], "shard", axis=0, tiled=True),
        lax.all_gather(params[11], "shard", axis=0, tiled=True),
    )
    (
        gain_one,
        bias_one,
        gain_two,
        bias_two,
        weight_qkv,
        bias_qkv,
        weight_out,
        bias_out,
        weight_up,
        bias_up,
        weight_down,
        bias_down,
    ) = gathered
    rows = hidden.shape[0]
    blk = rows // 2
    width = hidden.shape[1]
    order = block_order[0]
    places = positions[0]
    place_me = lax.axis_index("ctx")
    mine = lax.dynamic_slice(order, (2 * place_me,), (2,))
    offsets = jnp.arange(blk, dtype=jnp.int32)
    query_index = (mine[:, None] * blk + offsets[None, :]).reshape(-1)
    key_index = (order[:, None] * blk + offsets[None, :]).reshape(-1)
    query_start = query_index - places[query_index]
    key_start = key_index - places[key_index]
    allowed = (key_index[None, :] <= query_index[:, None]) & (
        key_start[None, :] == query_start[:, None]
    )
    cosine, sine = tables(places[query_index])
    scale = 1.0 / math.sqrt(HD)
    per_group = 2 * HD
    groups = width // per_group

    def split_groups(array):
        return array.reshape(array.shape[0], groups, per_group).swapaxes(0, 1)

    def join_groups(array):
        return array.swapaxes(0, 1).reshape(array.shape[1], groups * per_group)

    def group_scores(query_group, key_group):
        query_heads = query_group.reshape(query_group.shape[0], 2, HD)
        key_heads = key_group.reshape(key_group.shape[0], 2, HD)
        scores = (
            jnp.einsum("rhd,khd->hrk", query_heads, key_heads, preferred_element_type=jnp.float32)
            * scale
        )
        return (jnp.where(allowed[None], scores, -1e30), query_heads, key_heads)

    flat_in = hidden.astype(jnp.float32)
    normed_one = layer_norm(
        flat_in, gain_one.astype(jnp.float32), bias_one.astype(jnp.float32)
    ).astype(jnp.bfloat16)
    normed_two = layer_norm(
        flat_in, gain_two.astype(jnp.float32), bias_two.astype(jnp.float32)
    ).astype(jnp.bfloat16)
    joined = jnp.dot(normed_one, weight_qkv, preferred_element_type=jnp.float32) + bias_qkv.astype(
        jnp.float32
    )

    def rotate_rows(values):
        return rotate(values, cosine, sine)

    query_turned, query_back = jax.vjp(rotate_rows, joined[:, :width])
    key_turned, key_back = jax.vjp(rotate_rows, joined[:, width : 2 * width])
    query_b = query_turned.astype(jnp.bfloat16)
    key_b = key_turned.astype(jnp.bfloat16)
    value_b = joined[:, 2 * width :].astype(jnp.bfloat16)
    keys_all, values_all = (
        lax.all_gather(key_b, "ctx", axis=0, tiled=True),
        lax.all_gather(value_b, "ctx", axis=0, tiled=True),
    )

    def forward_group(inputs):
        query_group, key_group, value_group = inputs
        scores, query_heads, key_heads = group_scores(query_group, key_group)
        value_heads = value_group.reshape(value_group.shape[0], 2, HD)
        largest = jnp.max(scores, axis=-1, keepdims=True)
        weights = jnp.exp(scores - largest)
        total = jnp.sum(weights, axis=-1, keepdims=True)
        probs_b = (weights / total).astype(jnp.bfloat16)
        mixed_group = jnp.einsum(
            "hrk,khd->rhd", probs_b, value_heads, preferred_element_type=jnp.float32
        )
        log_total = largest[..., 0] + jnp.log(total[..., 0])
        return (mixed_group.reshape(query_group.shape[0], per_group), log_total)

    mixed_groups, log_totals = lax.map(
        forward_group, (split_groups(query_b), split_groups(keys_all), split_groups(values_all))
    )
    mixed = join_groups(mixed_groups).astype(jnp.bfloat16)
    branch_attn = jnp.dot(mixed, weight_out, preferred_element_type=jnp.float32) + bias_out.astype(
        jnp.float32
    )
    hidden_up = jnp.dot(normed_two, weight_up, preferred_element_type=jnp.float32) + bias_up.astype(
        jnp.float32
    )
    active_f, gelu_back = jax.vjp(exact_gelu, hidden_up)
    active = active_f.astype(jnp.bfloat16)
    branch_mlp = jnp.dot(
        active, weight_down, preferred_element_type=jnp.float32
    ) + bias_down.astype(jnp.float32)
    output = (flat_in + branch_attn + branch_mlp).astype(jnp.bfloat16)
    (
        gain_one,
        bias_one,
        gain_two,
        bias_two,
        weight_qkv,
        bias_qkv,
        weight_out,
        bias_out,
        weight_up,
        bias_up,
        weight_down,
        bias_down,
    ) = gathered
    cot_full = cotangent.astype(jnp.float32)
    grad_bias_out = jnp.sum(cot_full, axis=0)
    grad_bias_down = jnp.sum(cot_full, axis=0)
    grad_weight_down = jnp.dot(active.T, cotangent, preferred_element_type=jnp.float32)
    d_active = jnp.dot(cotangent, weight_down.T, preferred_element_type=jnp.float32)
    d_up = gelu_back(d_active)[0].astype(jnp.bfloat16)
    grad_bias_up = jnp.sum(d_up.astype(jnp.float32), axis=0)
    grad_weight_up = jnp.dot(normed_two.T, d_up, preferred_element_type=jnp.float32)
    d_two = jnp.dot(d_up, weight_up.T, preferred_element_type=jnp.float32)
    grad_weight_out = jnp.dot(mixed.T, cotangent, preferred_element_type=jnp.float32)
    d_mixed = jnp.dot(cotangent, weight_out.T, preferred_element_type=jnp.float32).astype(
        jnp.bfloat16
    )

    def make_backward():

        def backward_group(inputs):
            query_group, key_group, value_group, d_mixed_group, log_total = inputs
            scores, query_heads, key_heads = group_scores(query_group, key_group)
            value_heads = value_group.reshape(value_group.shape[0], 2, HD)
            d_heads = d_mixed_group.reshape(d_mixed_group.shape[0], 2, HD)
            probs = jnp.exp(scores - log_total[..., None])
            d_probs = jnp.einsum(
                "rhd,khd->hrk", d_heads, value_heads, preferred_element_type=jnp.float32
            )
            inner = jnp.sum(probs * d_probs, axis=-1, keepdims=True)
            d_scores = jnp.where(allowed[None], probs * (d_probs - inner), 0.0).astype(jnp.bfloat16)
            d_query = (
                jnp.einsum("hrk,khd->rhd", d_scores, key_heads, preferred_element_type=jnp.float32)
                * scale
            )
            d_query = d_query.reshape(query_group.shape[0], per_group)
            probs_b = probs.astype(jnp.bfloat16)
            d_key = (
                jnp.einsum(
                    "hrk,rhd->khd", d_scores, query_heads, preferred_element_type=jnp.float32
                )
                * scale
            )
            d_value = jnp.einsum(
                "hrk,rhd->khd", probs_b, d_heads, preferred_element_type=jnp.float32
            )
            return (
                d_query,
                d_key.reshape(key_group.shape[0], per_group),
                d_value.reshape(key_group.shape[0], per_group),
            )

        return backward_group

    group_inputs = (
        split_groups(query_b),
        split_groups(keys_all),
        split_groups(values_all),
        split_groups(d_mixed),
        log_totals,
    )
    d_query_groups, d_key_groups, d_value_groups = lax.map(make_backward(), group_inputs)
    d_key_mine, d_value_mine = (
        lax.psum_scatter(
            join_groups(d_key_groups).astype(jnp.bfloat16), "ctx", scatter_dimension=0, tiled=True
        ).astype(jnp.float32),
        lax.psum_scatter(
            join_groups(d_value_groups).astype(jnp.bfloat16), "ctx", scatter_dimension=0, tiled=True
        ).astype(jnp.float32),
    )
    d_query = query_back(join_groups(d_query_groups))[0]
    d_key = key_back(d_key_mine)[0]
    d_joined = jnp.concatenate([d_query, d_key, d_value_mine], axis=1).astype(jnp.bfloat16)
    grad_bias_qkv = jnp.sum(d_joined.astype(jnp.float32), axis=0)
    grad_weight_qkv = jnp.dot(normed_one.T, d_joined, preferred_element_type=jnp.float32)
    d_one = jnp.dot(d_joined, weight_qkv.T, preferred_element_type=jnp.float32)
    _, norm_one_back = jax.vjp(
        layer_norm, flat_in, gain_one.astype(jnp.float32), bias_one.astype(jnp.float32)
    )
    _, norm_two_back = jax.vjp(
        layer_norm, flat_in, gain_two.astype(jnp.float32), bias_two.astype(jnp.float32)
    )
    d_in_one, grad_gain_one, grad_bias_one = norm_one_back(d_one)
    d_in_two, grad_gain_two, grad_bias_two = norm_two_back(d_two)
    grad_input = cot_full + d_in_one + d_in_two
    grads = (
        grad_gain_one,
        grad_bias_one,
        grad_gain_two,
        grad_bias_two,
        grad_weight_qkv,
        grad_bias_qkv,
        grad_weight_out,
        grad_bias_out,
        grad_weight_up,
        grad_bias_up,
        grad_weight_down,
        grad_bias_down,
    )
    partial_sums = (
        lax.psum_scatter(
            grads[0].astype(jnp.bfloat16), "shard", scatter_dimension=0, tiled=True
        ).astype(jnp.float32),
        lax.psum_scatter(
            grads[1].astype(jnp.bfloat16), "shard", scatter_dimension=0, tiled=True
        ).astype(jnp.float32),
        lax.psum_scatter(
            grads[2].astype(jnp.bfloat16), "shard", scatter_dimension=0, tiled=True
        ).astype(jnp.float32),
        lax.psum_scatter(
            grads[3].astype(jnp.bfloat16), "shard", scatter_dimension=0, tiled=True
        ).astype(jnp.float32),
        lax.psum_scatter(
            grads[4].astype(jnp.bfloat16), "shard", scatter_dimension=0, tiled=True
        ).astype(jnp.float32),
        lax.psum_scatter(
            grads[5].astype(jnp.bfloat16), "shard", scatter_dimension=0, tiled=True
        ).astype(jnp.float32),
        lax.psum_scatter(
            grads[6].astype(jnp.bfloat16), "shard", scatter_dimension=0, tiled=True
        ).astype(jnp.float32),
        lax.psum_scatter(
            grads[7].astype(jnp.bfloat16), "shard", scatter_dimension=0, tiled=True
        ).astype(jnp.float32),
        lax.psum_scatter(
            grads[8].astype(jnp.bfloat16), "shard", scatter_dimension=0, tiled=True
        ).astype(jnp.float32),
        lax.psum_scatter(
            grads[9].astype(jnp.bfloat16), "shard", scatter_dimension=0, tiled=True
        ).astype(jnp.float32),
        lax.psum_scatter(
            grads[10].astype(jnp.bfloat16), "shard", scatter_dimension=0, tiled=True
        ).astype(jnp.float32),
        lax.psum_scatter(
            grads[11].astype(jnp.bfloat16), "shard", scatter_dimension=0, tiled=True
        ).astype(jnp.float32),
    )
    summed = (
        lax.psum(partial_sums[0].astype(jnp.bfloat16), "ctx").astype(jnp.float32),
        lax.psum(partial_sums[1].astype(jnp.bfloat16), "ctx").astype(jnp.float32),
        lax.psum(partial_sums[2].astype(jnp.bfloat16), "ctx").astype(jnp.float32),
        lax.psum(partial_sums[3].astype(jnp.bfloat16), "ctx").astype(jnp.float32),
        lax.psum(partial_sums[4].astype(jnp.bfloat16), "ctx").astype(jnp.float32),
        lax.psum(partial_sums[5].astype(jnp.bfloat16), "ctx").astype(jnp.float32),
        lax.psum(partial_sums[6].astype(jnp.bfloat16), "ctx").astype(jnp.float32),
        lax.psum(partial_sums[7].astype(jnp.bfloat16), "ctx").astype(jnp.float32),
        lax.psum(partial_sums[8].astype(jnp.bfloat16), "ctx").astype(jnp.float32),
        lax.psum(partial_sums[9].astype(jnp.bfloat16), "ctx").astype(jnp.float32),
        lax.psum(partial_sums[10].astype(jnp.bfloat16), "ctx").astype(jnp.float32),
        lax.psum(partial_sums[11].astype(jnp.bfloat16), "ctx").astype(jnp.float32),
    )
    return (
        output,
        grad_input,
        summed[0],
        summed[1],
        summed[2],
        summed[3],
        summed[4],
        summed[5],
        summed[6],
        summed[7],
        summed[8],
        summed[9],
        summed[10],
        summed[11],
    )


def solution(mesh):
    placed = (
        P(("shard", "ctx"), None),
        P("shard"),
        P("shard"),
        P("shard"),
        P("shard"),
        P("shard", None),
        P("shard"),
        P("shard", None),
        P("shard"),
        P("shard", None),
        P("shard"),
        P("shard", None),
        P("shard"),
        P("shard", None),
        P("shard", None),
        P(("shard", "ctx"), None),
    )
    return jax.shard_map(
        local,
        mesh=mesh,
        in_specs=placed,
        out_specs=(
            P(("shard", "ctx"), None),
            P(("shard", "ctx"), None),
            P("shard"),
            P("shard"),
            P("shard"),
            P("shard"),
            P("shard", None),
            P("shard"),
            P("shard", None),
            P("shard"),
            P("shard", None),
            P("shard"),
            P("shard", None),
            P("shard"),
        ),
        check_vma=False,
    )
```

profile of v0, /device:TPU:1, one launch (start us, length us, event | category | flops | bytes accessed | tf_op | source)
XLA Modules:
  0.0 885.4 jit_solution(14610380367349314064)
XLA Ops:
  15.6 16.1 %all-reduce.23 = (bf16[768]{0:T(1024)(128)(2,1)S(1)}, bf16[768]{0:T(1024)(128)(2,1)S(1)}, bf16[2304]{0:T(1024)(128)(2,1)S(1)}, bf16[768]{0:T(1024)(128)(2,1)S(1)}, bf16[768]{0:T(1024)(128)(2,1)S(1)}) all-reduce(bf16[768]{0:T(1024)(128)(2,1)S(1)} %dynamic-update-slice.5, ...), channel_id=1, replica_groups=mesh['ctx'=32,'shard'=4] {'shard'}, use_global_device_ids=true, to_apply=%add.11 | all-reduce | flops 5376 | bytes 21504
  33.0 23.1 %all-gather.8.cloned.1.call-done = bf16[768,2304]{1,0:T(8,128)(2,1)} async-done(((bf16[192,2304]{1,0:T(8,128)(2,1)}), bf16[768,2304]{1,0:T(8,128)(2,1)}) %all-gather.8.cloned.1.call-update) | async-done | bytes 3538960 | tf_op jit(solution)/shard_map/all_gather | solution.py:79
  56.2 2.7 convolution_add_fusion
  64.3 23.0 %gather_fusion = s32[4096]{0:T(1024)S(1)} fusion(s32[4096]{0:T(1024)S(1)} %bitcast.165, s32[4096]{0:T(1024)S(1)} %broadcast_clamp_fusion), kind=kCustom, calls=%fused_computation | custom fusion | bytes 49152 | tf_op jit(solution)/shard_map/gather | solution.py:113
  87.3 1.8 convolution_convert_fusion.4
  90.0 45.1 %all-gather.10.cloned.1.call-done = bf16[4096,768]{1,0:T(8,128)(2,1)} async-done(((bf16[128,768]{1,0:T(8,128)(2,1)}), bf16[4096,768]{1,0:T(8,128)(2,1)}) %all-gather.10.cloned.1.call-update) | async-done | bytes 6291472 | tf_op jit(solution)/shard_map/all_gather | solution.py:158
  135.1 8.7 copy.44
  143.9 47.2 %all-gather.12.cloned.1.call-done = bf16[4096,768]{0,1:T(8,128)(2,1)} async-done(((bf16[128,768]{0,1:T(8,128)(2,1)}), bf16[4096,768]{0,1:T(8,128)(2,1)}) %all-gather.12.cloned.1.call-update) | async-done | bytes 6291472 | tf_op jit(solution)/shard_map/all_gather | solution.py:157
  191.0 30.9 %while.30 = (s32[]{:T(128)}, bf16[6,128,128]{1,2,0:T(8,128)(2,1)S(1)}, f32[6,2,128]{2,1,0:T(2,128)S(1)}, bf16[6,4096,128]{1,2,0:T(8,128)(2,1)}, bf16[6,128,128]{...) while((s32[]{:T(128)}, ...), condition=%wide.region_5.6_spmd.clone.clone, body=%wide.region_2.5_spmd.clone.sunk.clone | while | flops 278396672 | bytes 20161660 | solution.py:175
  196.1 1.7 constant_dynamic-slice_fusion.20
  201.2 1.9 constant_dynamic-slice_fusion.20
  206.6 1.7 constant_dynamic-slice_fusion.20
  216.8 1.7 constant_dynamic-slice_fusion.20
  221.9 175.2 %while.31 = (s32[]{:T(128)}, f32[6,128,128]{1,2,0:T(8,128)}, bf16[6,4096,128]{1,2,0:T(8,128)(2,1)}, bf16[6,4096,128]{1,2,0:T(8,128)(2,1)}, bf16[6,4096,128]{1,2,...) while((s32[]{:T(128)}, f32[6,128,128]{1,2,0:T(8,128)}, ...), condition=%wide.region_8.9_spmd.clone.clone, body=%wide.region_6.8_spmd.clone.sunk.clone | while | flops 688415232 | bytes 45584544 | solution.py:262
  223.8 3.3 fusion.166
  229.1 2.8 fusion.167
  231.9 7.2 fusion.168
  239.7 2.6 fusion.169
  242.4 7.3 convolution_multiply_fusion.5
  252.9 3.3 fusion.166
  258.3 2.8 fusion.167
  261.2 7.2 fusion.168
  269.0 2.6 fusion.169
  271.6 7.4 convolution_multiply_fusion.5
  282.5 3.3 fusion.166
  287.8 2.8 fusion.167
  290.6 7.1 fusion.168
  298.4 2.6 fusion.169
  301.0 7.3 convolution_multiply_fusion.5
  311.6 3.3 fusion.166
  316.9 2.8 fusion.167
  319.7 7.1 fusion.168
  327.5 2.6 fusion.169
  330.1 7.3 convolution_multiply_fusion.5
  340.7 3.3 fusion.166
  346.0 2.8 fusion.167
  348.8 7.1 fusion.168
  356.6 2.6 fusion.169
  359.2 7.3 convolution_multiply_fusion.5
  369.8 3.3 fusion.166
  375.2 2.8 fusion.167
  378.0 7.1 fusion.168
  385.7 2.6 fusion.169
  388.3 7.3 convolution_multiply_fusion.5
  397.2 8.6 copy.48
  405.9 8.6 copy.50
  415.2 9.7 %all-gather = bf16[4,1,768]{2,1,0:T(2,128)(2,1)S(1)} all-gather(bf16[1,1,768]{2,1,0:T(2,128)(2,1)S(1)} %reshape.413), channel_id=1, replica_groups=mesh['ctx'=32,'shard'=4] {'shard'}, dimensions={0}, use_global_device_ids=true | all-gather | bytes 7680 | tf_op jit(solution)/shard_map/all_gather | solution.py:84
  424.9 3.4 convolution_add_fusion.1
  428.3 8.2 fusion.71
  437.4 3.7 convolution_convert_fusion.1
  442.7 3.6 convolution_convert_fusion
  449.0 40.7 %reduce-scatter.19.cloned.1.call-done = bf16[128,768]{1,0:T(8,128)(2,1)} async-done(((bf16[4096,768]{1,0:T(8,128)(2,1)}), bf16[128,768]{1,0:T(8,128)(2,1)}) %reduce-scatter.19.cloned.1.call-update) | async-done | bytes 196624
  490.8 88.6 %reduce-scatter.21.cloned.1.call-done = bf16[128,768]{1,0:T(8,128)(2,1)} async-done(((bf16[4096,768]{1,0:T(8,128)(2,1)}), bf16[128,768]{1,0:T(8,128)(2,1)}) %reduce-scatter.21.cloned.1.call-update) | async-done | bytes 196624
  581.4 3.1 convolution_convert_fusion.2
  587.4 4.2 fusion.78
  593.3 40.9 %reduce-scatter.15.cloned.1.call-done = bf16[192,3072]{1,0:T(8,128)(2,1)} async-done(((bf16[768,3072]{1,0:T(8,128)(2,1)}), bf16[192,3072]{1,0:T(8,128)(2,1)}) %reduce-scatter.15.cloned.1.call-update) | async-done | bytes 1179664 | tf_op jit(solution)/shard_map/reduce_scatter | solution.py:325
  634.3 53.2 %reduce-scatter.17.cloned.1.call-done = bf16[768,768]{1,0:T(8,128)(2,1)} async-done(((bf16[3072,768]{1,0:T(8,128)(2,1)}), bf16[768,768]{1,0:T(8,128)(2,1)}) %reduce-scatter.17.cloned.1.call-update) | async-done | bytes 1179664 | tf_op jit(solution)/shard_map/reduce_scatter | solution.py:331
  687.4 25.8 %reduce-scatter.13.cloned.1.call-done = bf16[192,768]{1,0:T(8,128)(2,1)} async-done(((bf16[768,768]{1,0:T(8,128)(2,1)}), bf16[192,768]{1,0:T(8,128)(2,1)}) %reduce-scatter.13.cloned.1.call-update) | async-done | bytes 294928 | tf_op jit(solution)/shard_map/reduce_scatter | solution.py:319
  713.2 44.7 %reduce-scatter.11.cloned.1.call-done = bf16[192,2304]{1,0:T(8,128)(2,1)} async-done(((bf16[768,2304]{1,0:T(8,128)(2,1)}), bf16[192,2304]{1,0:T(8,128)(2,1)}) %reduce-scatter.11.cloned.1.call-update) | async-done | bytes 884752 | tf_op jit(solution)/shard_map/reduce_scatter | solution.py:313
  758.4 11.3 %all-reduce.22 = (bf16[768]{0:T(1024)(128)(2,1)S(1)}, bf16[768]{0:T(1024)(128)(2,1)S(1)}, bf16[768]{0:T(1024)(128)(2,1)S(1)}, bf16[768]{0:T(1024)(128)(2,1)S(1)}...) all-reduce(bf16[768]{0:T(1024)(128)(2,1)S(1)} %dynamic-update-slice, ...), channel_id=1, replica_groups=mesh['ctx'=32,'shard'=4] {'shard'}, use_global_device_ids=true, to_apply=%add.12 | all-reduce | flops 10752 | bytes 43008
  770.2 67.5 %all-reduce.20 = (bf16[192]{0:T(256)(128)(2,1)S(1)}, bf16[192]{0:T(256)(128)(2,1)S(1)}, bf16[192]{0:T(256)(128)(2,1)S(1)}, bf16[192]{0:T(256)(128)(2,1)S(1)}, bf...) all-reduce(bf16[192]{0:T(256)(128)(2,1)S(1)} %dynamic-slice.9, ...), channel_id=1, replica_groups=mesh['ctx'=32,'shard'=4] {'ctx'}, use_global_device_ids=true, to_apply=%region_17.18 | all-reduce | flops 2304 | bytes 9216 | tf_op jit(solution)/shard_map/psum | solution.py:339
  842.2 3.2 convolution_add_fusion.3
  846.5 25.1 %all-reduce.26.cloned.1.call-done = (bf16[192,2304]{1,0:T(8,128)(2,1)}, bf16[192,768]{1,0:T(8,128)(2,1)}, bf16[192,3072]{1,0:T(8,128)(2,1)}, bf16[768,768]{1,0:T(8,128)(2,1)}) async-done(((bf16[192,2304]{1,0:T(8,128)(2,1)}, bf16[192,768]{1,0:T(8,128)(2,1)}, bf16[192,3072]{1,0:T(8,128)(2,1)}, bf16[768,768]{1,0:T(8,128)(2,1)}), (bf16[192,2304]{1,0:T(8,128)(2,1)}, bf16[192,768]{1,0:T(8,128)(2,1)}, ...) | async-done | bytes 3538960 | tf_op jit(solution)/shard_map/psum | solution.py:343
  871.6 2.6 convert_element_type.231
  (254 shorter events, 96.8 us)
Async XLA Ops:
  7.2 52.8 %copy-start = (s32[1,4096]{1,0:T(1,128)S(1)}, s32[1,4096]{1,0:T(1,128)}, u32[]{:S(2)}) copy-start(s32[1,4096]{1,0:T(1,128)} %param.34) | copy-start | bytes 49156
  7.2 25.6 %copy-start.2 = (bf16[128,768]{1,0:T(8,128)(2,1)S(1)}, bf16[128,768]{1,0:T(8,128)(2,1)}, u32[]{:S(2)}) copy-start(bf16[128,768]{1,0:T(8,128)(2,1)} %param.20) | copy-start | bytes 589828
  7.2 49.0 %all-gather.8.cloned.1.call-start = ((), (), s32[]{:S(2)}) async-start(), calls=%async_computation.6 | async-start | bytes 4423680 | tf_op jit(solution)/shard_map/all_gather | solution.py:79
  7.9 79.4 %all-gather.14.cloned.1.call-start = ((), (), s32[]{:S(2)}) async-start(), calls=%async_computation.9 | async-start | bytes 1474560 | tf_op jit(solution)/shard_map/all_gather | solution.py:81
  8.7 126.5 %all-gather.10.cloned.1.call-start = ((), (), s32[]{:S(2)}) async-start(), calls=%async_computation.7 | async-start | bytes 6488064 | tf_op jit(solution)/shard_map/all_gather | solution.py:158
  33.0 25.9 %copy-start.11 = (f32[128]{0:T(128)}, f32[128]{0:T(128)S(1)}, u32[]{:S(2)}) copy-start(f32[128]{0:T(128)S(1)} %fusion.56) | copy-start | bytes 1540
  33.0 26.6 %copy-start.15 = (s32[1,64]{1,0:T(1,128)S(1)}, s32[1,64]{1,0:T(1,128)}, u32[]{:S(2)}) copy-start(s32[1,64]{1,0:T(1,128)} %param.33) | copy-start | bytes 772
  59.6 131.4 %all-gather.12.cloned.1.call-start = ((), (), s32[]{:S(2)}) async-start(), calls=%async_computation.8 | async-start | bytes 6488064 | tf_op jit(solution)/shard_map/all_gather | solution.py:157
  62.5 362.4 %all-gather.16.cloned.1.call-start = ((), (), s32[]{:S(2)}) async-start(), calls=%async_computation.10 | async-start | bytes 5898240 | tf_op jit(solution)/shard_map/all_gather | solution.py:83
  63.1 365.3 %all-gather.18.cloned.1.call-start = ((), (), s32[]{:S(2)}) async-start(), calls=%async_computation.11 | async-start | bytes 5898240 | tf_op jit(solution)/shard_map/all_gather | solution.py:85
  63.6 426.0 %reduce-scatter.19.cloned.1.call-start = ((), (), s32[]{:S(2)}) async-start(), calls=%async_computation.16 | async-start | bytes 6488064
  64.2 23.1 %copy-start.3 = (bf16[128,768]{1,0:T(8,128)(2,1)S(1)}, bf16[128,768]{1,0:T(8,128)(2,1)}, u32[]{:S(2)}) copy-start(bf16[128,768]{1,0:T(8,128)(2,1)} %param.35) | copy-start | bytes 589828
  405.8 173.6 %reduce-scatter.21.cloned.1.call-start = ((), (), s32[]{:S(2)}) async-start(), calls=%async_computation.17 | async-start | bytes 6488064
  414.5 0.7 copy-start.13
  414.5 219.7 %reduce-scatter.15.cloned.1.call-start = ((), (), s32[]{:S(2)}) async-start(), calls=%async_computation.14 | async-start | bytes 5898240 | tf_op jit(solution)/shard_map/reduce_scatter | solution.py:325
  436.5 0.9 copy-start.6
  441.1 246.4 %reduce-scatter.17.cloned.1.call-start = ((), (), s32[]{:S(2)}) async-start(), calls=%async_computation.15 | async-start | bytes 5898240 | tf_op jit(solution)/shard_map/reduce_scatter | solution.py:331
  446.4 266.9 %reduce-scatter.13.cloned.1.call-start = ((), (), s32[]{:S(2)}) async-start(), calls=%async_computation.13 | async-start | bytes 1474560 | tf_op jit(solution)/shard_map/reduce_scatter | solution.py:319
  447.9 310.0 %reduce-scatter.11.cloned.1.call-start = ((), (), s32[]{:S(2)}) async-start(), calls=%async_computation.12 | async-start | bytes 4423680 | tf_op jit(solution)/shard_map/reduce_scatter | solution.py:313
  584.6 2.4 copy-start.16
  584.6 2.6 copy-start.17
  584.6 2.8 copy-start.7
  584.6 287.0 %all-reduce.26.cloned.1.call-start = ((), (), s32[]{:S(2)}) async-start(), calls=%async_computation.18 | async-start | bytes 7077888 | tf_op jit(solution)/shard_map/psum | solution.py:343
  587.4 4.4 copy-start.5
  591.8 1.5 copy-start.12
  840.6 37.8 %copy-start.14 = (f32[192]{0:T(256)}, f32[192]{0:T(256)S(1)}, u32[]{:S(2)}) copy-start(f32[192]{0:T(256)S(1)} %convert_element_type.235) | copy-start | bytes 2308
  842.2 3.2 copy-start.4
  871.6 2.6 copy-start.10
  871.6 3.5 copy-start.9
  875.1 1.7 copy-start.8
  876.8 2.1 copy-start.1
Sparse Core Ops, SparseCore 0:
  9.7 46.4 all-gather.7
  57.8 23.6 all-gather.13
  84.3 50.7 all-gather.9
  137.8 53.2 all-gather.11
  192.5 52.1 all-gather.15
  246.2 53.0 all-gather.17
  406.0 83.6 reduce-scatter.18
  493.8 85.5 reduce-scatter.20
  581.8 52.3 reduce-scatter.14
  636.5 50.8 reduce-scatter.16
  690.4 22.7 reduce-scatter.12
  715.5 42.3 reduce-scatter.10
  761.6 109.9 all-reduce.25
where the time goes:
time: 888 us; the launch traced here: 885 us
  waiting for transfers between devices  437 us (49%)
  matrix products  190 us (21%)
  local copies, waits for them, and re-layouts  108 us (12%)
  blocking collectives  105 us (12%)
  other arithmetic  27.1 us (3%)
  between operations  17.7 us (2%)
    unnamed x15, waiting for transfers between devices  132 us
    psum x1, blocking collectives, local(): lax.psum(partial_sums[0].astype(jnp.bfloat16), 'ctx').astype(jnp.float32)  67.5 us
    reduce_scatter x1, waiting for transfers between devices, local(): lax.psum_scatter(grads[10].astype(jnp.bfloat16), 'shard', scatter_dimensi...  53.2 us
    all_gather x1, waiting for transfers between devices, local(): lax.all_gather(key_b, 'ctx', axis=0, tiled=True)  47.2 us
    all_gather x1, waiting for transfers between devices, local(): lax.all_gather(value_b, 'ctx', axis=0, tiled=True)  45.1 us
    reduce_scatter x1, waiting for transfers between devices, local(): lax.psum_scatter(grads[4].astype(jnp.bfloat16), 'shard', scatter_dimensio...  44.7 us
    dot_general x6, matrix products, backward_group(): jnp.einsum('hrk,rhd->khd', d_scores, query_heads, preferred_element_type=...  43.9 us
    dot_general x6, matrix products, backward_group(): jnp.einsum('hrk,khd->rhd', d_scores, key_heads, preferred_element_type=jn...  42.8 us
  transfers between devices with their start and end apart: 13, of which 10 were waited for; matrix products, arithmetic and copies ran while one was open for 36% of the time, Pallas kernels for 0%

commit v1 on v0

v1 whole, which is shorter than its diff:
```python
import functools
import math

import jax
import jax.numpy as jnp
import numpy as np
from jax import lax
from jax.experimental import pallas as pl
from jax.experimental.pallas import tpu as pltpu
from jax.sharding import PartitionSpec as P

HD = 64
ROT = 16
D = 768
NH = 3
HC = NH * HD
CHUNK = 512
MESH = pl.DeviceIdType.MESH
BF = jnp.bfloat16
F32 = jnp.float32
LIMIT = 56 * 1024 * 1024


def vmem(count):
    return [pl.BlockSpec(memory_space=pltpu.VMEM)] * count


def spots():
    c = lax.axis_index("ctx")
    return c, lax.div(c, 8), lax.rem(lax.div(c, 2), 4), lax.rem(c, 2)


def place(y, x, k):
    return y * 8 + x * 2 + k


def send(src, dst, send_sem, recv_sem, where):
    copy = pltpu.make_async_remote_copy(
        src_ref=src,
        dst_ref=dst,
        send_sem=send_sem,
        recv_sem=recv_sem,
        device_id=where,
        device_id_type=MESH,
    )
    copy.start()
    return copy


def greet(peers):
    barrier = pltpu.get_barrier_semaphore()
    for peer in peers:
        pl.semaphore_signal(barrier, inc=1, device_id=peer, device_id_type=MESH)
    pl.semaphore_wait(barrier, len(peers))


def dma(*dims):
    return pltpu.SemaphoreType.DMA(dims)


def params(ident):
    return pltpu.CompilerParams(
        collective_id=ident, has_side_effects=True, vmem_limit_bytes=LIMIT
    )


def spread_kernel(
    hid, cot, w_qkv, wu, g1, b1, g2, b2, bo, bd, bq, meta,
    h_all, c_all, wq_all, wu_all, s_all, m_all,
    wq, small, so, ro, sp, rp, sf, rf, ss, rs,
):
    z = lax.axis_index("shard")
    c, y, x, k = spots()
    sibling = {"ctx": c + 1 - 2 * k}
    peers = [{"shard": lax.rem(z + d, 4)} for d in range(4)]
    greet(peers[1:] + [sibling])
    rows = wu.shape[0]
    half = rows // 2
    width = wu_all.shape[2]
    for p in range(4):
        wq[p] = jnp.concatenate(
            [w_qkv[:, D * t + HC * p : D * t + HC * p + HC] for t in range(3)], axis=1
        )
    small[...] = jnp.zeros_like(small)
    for i, ref in enumerate((g1, b1, g2, b2, bo, bd)):
        small[i : i + 1] = ref[...].astype(F32)
    small[6:9] = bq[...].astype(F32)

    mine = pl.ds(pl.multiple_of(k * half, 16), half)
    weights, others = {}, []
    for d in (1, 3, 2):
        p = lax.rem(z + d, 4)
        cols = pl.ds(pl.multiple_of(p * width, 128), width)
        weights[d] = [
            send(wq.at[p, mine], wq_all.at[z, mine], sp.at[0, d - 1], rp.at[0, d - 1], peers[d]),
            send(wu.at[mine, cols], wu_all.at[z, mine], sp.at[1, d - 1], rp.at[1, d - 1], peers[d]),
        ]
    cut = hid.shape[0] // 2
    parts = [pl.ds(0, cut), pl.ds(cut, cut)]
    ring = {}
    for i, (src, dst) in enumerate(((hid, h_all), (cot, c_all))):
        for n in range(2):
            ring[i, 1, n] = send(
                src.at[parts[n]], dst.at[z, parts[n]], so.at[i, 0, n], ro.at[i, 0, n], peers[1]
            )
            m = 1 - n
            ring[i, 3, m] = send(
                src.at[parts[m]], dst.at[z, parts[m]], so.at[i, 1, m], ro.at[i, 1, m], peers[3]
            )
    for d in (1, 2, 3):
        for i, (src, dst) in enumerate(((small, s_all), (meta, m_all))):
            others.append(send(src, dst.at[z], ss.at[i, d - 1], rs.at[i, d - 1], peers[d]))
    h_all[z] = hid[...]
    c_all[z] = cot[...]
    s_all[z] = small[...]
    m_all[z] = meta[...]
    wq_all[z] = wq[z]
    wu_all[z] = wu[:, pl.ds(pl.multiple_of(z * width, 128), width)]
    before, after = lax.rem(z + 3, 4), lax.rem(z + 1, 4)
    for d in (1, 3, 2):
        source = lax.rem(z + 4 - d, 4)
        for i, full in enumerate((wq_all, wu_all)):
            weights[d][i].wait_recv()
            part = full.at[source, mine]
            others.append(send(part, part, sf.at[i, d - 1], rf.at[i, d - 1], sibling))
    for i, full in enumerate((h_all, c_all)):
        ring[i, 1, 0].wait_recv()
        part = full.at[before, parts[0]]
        others.append(send(part, part, ss.at[2 + i, 0], rs.at[2 + i, 0], peers[1]))
        ring[i, 3, 1].wait_recv()
        part = full.at[after, parts[1]]
        others.append(send(part, part, ss.at[2 + i, 1], rs.at[2 + i, 1], peers[3]))
    for i in range(2):
        ring[i, 1, 1].wait_recv()
        ring[i, 3, 0].wait_recv()
    for copy in others:
        copy.wait()
    for d in (1, 3, 2):
        for copy in weights[d]:
            copy.wait_send()
    for copy in ring.values():
        copy.wait_send()


def spread(hid, cot, w_qkv, wu, vectors, meta):
    rows = hid.shape[0]
    width = wu.shape[1] // 4
    return pl.pallas_call(
        spread_kernel,
        out_shape=(
            jax.ShapeDtypeStruct((4, rows, D), BF),
            jax.ShapeDtypeStruct((4, rows, D), BF),
            jax.ShapeDtypeStruct((4, wu.shape[0], 3 * HC), BF),
            jax.ShapeDtypeStruct((4, wu.shape[0], width), BF),
            jax.ShapeDtypeStruct((4, 16, HC), F32),
            jax.ShapeDtypeStruct((4,) + meta.shape, jnp.int32),
        ),
        in_specs=vmem(12),
        out_specs=tuple(vmem(6)),
        scratch_shapes=[
            pltpu.VMEM((4, wu.shape[0], 3 * HC), BF),
            pltpu.VMEM((16, HC), F32),
            dma(2, 2, 2), dma(2, 2, 2), dma(2, 3), dma(2, 3), dma(2, 3), dma(2, 3),
            dma(4, 3), dma(4, 3),
        ],
        compiler_params=params(0),
    )(hid, cot, w_qkv, wu, *vectors, meta)


def dot(left, right):
    return jnp.dot(left, right, preferred_element_type=F32)


def dot_nt(left, right):
    return lax.dot_general(left, right, (((1,), (1,)), ((), ())), preferred_element_type=F32)


def dot_tn(left, right):
    return lax.dot_general(left, right, (((0,), (0,)), ((), ())), preferred_element_type=F32)


def normalize(flat):
    center = flat - jnp.mean(flat, axis=-1, keepdims=True)
    r = lax.rsqrt(jnp.mean(center * center, axis=-1, keepdims=True) + 1e-05)
    return center * r, r


def vector(s_all, i):
    return jnp.concatenate([s_all[p, i : i + 1] for p in range(4)], axis=1)


def turned(v, cosine, sine):
    first, second = v[0:8], v[8:16]
    return jnp.concatenate(
        [first * cosine - second * sine, second * cosine + first * sine, v[16:]], axis=0
    )


def project_kernel(h_all, c_all, wq, s_all, cs, w_out, qkvd, normed):
    z = lax.axis_index("shard")
    count = h_all.shape[1]
    xhat, _ = normalize(h_all[...].reshape(4 * count, D).astype(F32))
    n1 = (xhat * vector(s_all, 0) + vector(s_all, 1)).astype(BF)
    normed[...] = n1
    bias = []
    for t in range(3):
        piece = jnp.zeros((1, HC), F32)
        for p in range(4):
            n = 4 * t + p
            piece = piece + jnp.where(z == p, s_all[n // 3, 6 + n % 3 : 7 + n % 3], 0.0)
        bias.append(piece)
    joined = dot(n1, wq[...].reshape(D, 3 * HC)) + jnp.concatenate(bias, axis=1)
    d_mixed = dot_nt(w_out[...], c_all[...].reshape(4 * count, D)).astype(BF)
    for s in range(4):
        jt = joined[count * s : count * s + count].T
        cosine, sine = cs[s, 0:8], cs[s, 8:16]
        for h in range(NH):
            at = HD * h
            qkvd[s, at : at + HD] = turned(jt[HC + at : HC + at + HD], cosine, sine).astype(BF)
            qkvd[s, 2 * HC + at : 2 * HC + at + HD] = turned(jt[at : at + HD], cosine, sine).astype(BF)
        qkvd[s, HC : 2 * HC] = jt[2 * HC :].astype(BF)
        qkvd[s, 3 * HC :] = d_mixed[:, count * s : count * s + count]


def project(h_all, c_all, wq, s_all, cs, w_out):
    count = h_all.shape[1]
    return pl.pallas_call(
        project_kernel,
        out_shape=(
            jax.ShapeDtypeStruct((4, 4 * HC, count), BF),
            jax.ShapeDtypeStruct((4 * count, D), BF),
        ),
        in_specs=vmem(6),
        out_specs=tuple(vmem(2)),
        compiler_params=pltpu.CompilerParams(vmem_limit_bytes=LIMIT),
    )(h_all, c_all, wq, s_all, cs, w_out)


def feed_kernel(h_all, c_all, wu, w_down, s_all, b_up, zpart, g_up, g_down, small):
    count = h_all.shape[1]
    xhat, _ = normalize(h_all[...].reshape(4 * count, D).astype(F32))
    n2 = (xhat * vector(s_all, 2) + vector(s_all, 3)).astype(BF)
    up = wu[...].reshape(D, wu.shape[2])
    cot = c_all[...].reshape(4 * count, D)
    hidden = dot(n2, up) + b_up[...]
    rise = 0.5 * (1.0 + lax.erf(hidden * (1.0 / math.sqrt(2.0))))
    slope = rise + hidden * jnp.exp(-0.5 * hidden * hidden) * (1.0 / math.sqrt(2.0 * math.pi))
    active = (hidden * rise).astype(BF)
    d_up_f = (dot_nt(cot, w_down[...]) * slope).astype(BF)
    g_down[...] = dot_tn(active, cot).astype(BF)
    g_up[...] = dot_tn(n2, d_up_f).astype(BF).reshape(g_up.shape)
    branch = dot(active, w_down[...]).astype(BF)
    d_two = dot_nt(d_up_f, up)
    for s in range(4):
        zpart[s, 0] = branch[count * s : count * s + count]
        zpart[s, 1] = d_two[count * s : count * s + count].astype(BF)
    small[...] = jnp.zeros_like(small)
    small[2:3] = jnp.sum(d_two * xhat, axis=0, keepdims=True)
    small[3:4] = jnp.sum(d_two, axis=0, keepdims=True)
    small[4:5] = jnp.sum(cot.astype(F32), axis=0, keepdims=True)
    small[5:6] = jnp.sum(d_up_f.astype(F32), axis=0, keepdims=True)


def feed(h_all, c_all, wu, w_down, s_all, b_up):
    count = h_all.shape[1]
    return pl.pallas_call(
        feed_kernel,
        out_shape=(
            jax.ShapeDtypeStruct((4, 2, count, D), BF),
            jax.ShapeDtypeStruct(wu.shape, BF),
            jax.ShapeDtypeStruct(w_down.shape, BF),
            jax.ShapeDtypeStruct((8, D), F32),
        ),
        in_specs=vmem(6),
        out_specs=tuple(vmem(4)),
        compiler_params=pltpu.CompilerParams(vmem_limit_bytes=LIMIT),
    )(h_all, c_all, wu, w_down, s_all, b_up)


def gather_kernel(
    qkvd, g_up, kv_all, qd_all, u_all, sa, ra, sq, rq, sb, rb, sd, rd, sc, rc, sz, rz
):
    z = lax.axis_index("shard")
    c, y, x, k = spots()
    half = kv_all.shape[1]
    base = x * 8 + k * 4
    sibling = {"ctx": c + 1 - 2 * k}
    y_peer = [{"ctx": place(lax.rem(y + d, 4), x, k)} for d in range(4)]
    x_peer = [{"ctx": place(y, lax.rem(x + d, 4), k)} for d in (0, 1, 3)]
    z_peer = [{"shard": lax.rem(z + d, 4)} for d in range(4)]
    greet(y_peer[1:] + x_peer[1:] + z_peer[1:] + [sibling])
    first, tail = {}, []
    for d in (1, 3, 2):
        yp = lax.rem(y + d, 4)
        first[d] = send(
            qkvd.at[yp, pl.ds(0, half)], kv_all.at[base + y], sa.at[d - 1], ra.at[d - 1], y_peer[d]
        )
    for d in (1, 3, 2):
        zp = lax.rem(z + d, 4)
        tail.append(send(g_up.at[zp], u_all.at[z], sz.at[d - 1], rz.at[d - 1], z_peer[d]))
    kv_all[base + y] = qkvd[y, 0:half]
    u_all[z] = g_up[z]
    across = {}
    for d in (0, 1, 3, 2):
        ys = lax.rem(y + 4 - d, 4)
        if d:
            first[d].wait_recv()
        block = kv_all.at[base + ys]
        for e in (1, 2):
            across[d, e] = send(block, block, sb.at[d, e], rb.at[d, e], x_peer[e])
        across[d, 0] = send(block, block, sb.at[d, 0], rb.at[d, 0], sibling)
    for d in (1, 3, 2):
        yp = lax.rem(y + d, 4)
        tail.append(
            send(qkvd.at[yp, pl.ds(half, half)], qd_all.at[y], sq.at[d - 1], rq.at[d - 1], y_peer[d])
        )
    qd_all[y] = qkvd[y, half:]
    relay = {}
    for d in (0, 1, 3, 2):
        ys = lax.rem(y + 4 - d, 4)
        for e in (1, 2):
            across[d, e].wait_recv()
            block = kv_all.at[lax.rem(x + 4 - (1, 3)[e - 1], 4) * 8 + k * 4 + ys]
            if e == 1 + d // 2:
                relay[d] = send(block, block, sd.at[d], rd.at[d], x_peer[e])
            tail.append(send(block, block, sc.at[d, e], rc.at[d, e], sibling))
    for d in (0, 1, 3, 2):
        ys = lax.rem(y + 4 - d, 4)
        relay[d].wait_recv()
        block = kv_all.at[lax.rem(x + 2, 4) * 8 + k * 4 + ys]
        tail.append(send(block, block, sc.at[d, 0], rc.at[d, 0], sibling))
    for copy in tail:
        copy.wait()
    for d in range(4):
        across[d, 0].wait_recv()
        relay[d].wait_send()
        for e in range(3):
            across[d, e].wait_send()
        if d:
            first[d].wait_send()


def gather(qkvd, g_up):
    _, rows, cols = qkvd.shape
    return pl.pallas_call(
        gather_kernel,
        out_shape=(
            jax.ShapeDtypeStruct((32, rows // 2, cols), BF),
            jax.ShapeDtypeStruct((4, rows // 2, cols), BF),
            jax.ShapeDtypeStruct(g_up.shape, BF),
        ),
        in_specs=vmem(2),
        out_specs=tuple(vmem(3)),
        scratch_shapes=[
            dma(3), dma(3), dma(3), dma(3), dma(4, 3), dma(4, 3), dma(4), dma(4),
            dma(4, 3), dma(4, 3), dma(3), dma(3),
        ],
        compiler_params=params(1),
    )(qkvd, g_up)


def attention_kernel(
    nums, kv_all, qd_all, t_q, s_q, d_kv, o_q, kt, vt, dkt, dvt, qdt, oqt, s_buf, p_buf
):
    lane = lax.broadcasted_iota(jnp.int32, (2 * HC, 128), 1)
    left = lane < 64

    def pair(j):
        b0, b1 = 2 * j, 2 * j + 1
        return nums[b0], nums[b1], nums[32 + b0], nums[32 + b1]

    def sort(j, carry):
        slot0, slot1, f0, f1 = pair(j)
        one = pltpu.roll(kv_all[slot0].astype(F32), 64 * f0, 1)
        two = pltpu.roll(kv_all[slot1].astype(F32), 64 * (1 - f1), 1)
        low = jnp.where(left, one, two).astype(BF)
        high = jnp.where(left, two, one).astype(BF)
        at_low = pl.ds(pl.multiple_of(j * 128, 128), 128)
        at_high = pl.ds(pl.multiple_of((31 - j) * 128, 128), 128)
        kt[:, at_low] = low[:HC]
        vt[:, at_low] = low[HC:]
        kt[:, at_high] = high[:HC]
        vt[:, at_high] = high[HC:]
        return carry

    lax.fori_loop(0, 16, sort, 0)
    dkt[...] = jnp.zeros_like(dkt)
    dvt[...] = jnp.zeros_like(dvt)
    for g in range(2):
        one = pltpu.roll(qd_all[2 * g].astype(F32), 64 * nums[64 + 2 * g], 1)
        two = pltpu.roll(qd_all[2 * g + 1].astype(F32), 64 * nums[65 + 2 * g], 1)
        cols = slice(128 * g, 128 * g + 128)
        qdt[0, :, cols] = jnp.where(left, one, pltpu.roll(two, 64, 1))
        qdt[1, :, cols] = jnp.where(left, pltpu.roll(one, 64, 1), two)

    def one_head(tile, h):
        lo, hi = nums[68 + 2 * tile], nums[69 + 2 * tile]
        rows = slice(HD * h, HD * h + HD)
        q_t = qdt[tile, rows, :] * 0.125
        d_t = qdt[tile, HC + HD * h : HC + HD * h + HD, :]
        q_n = q_t.T.astype(BF)
        d_n = d_t.T.astype(BF)
        q_t = q_t.astype(BF)
        d_t = d_t.astype(BF)
        first = s_q[tile]
        last = t_q[tile]

        def scores(i, top):
            at = pl.ds(pl.multiple_of(i * CHUNK, CHUNK), CHUNK)
            s = dot(q_n, kt[rows, at])
            key = lax.broadcasted_iota(jnp.int32, s.shape, 1) + i * CHUNK
            s = jnp.where((key >= first) & (key <= last), s, -1e30)
            s_buf[:, at] = s
            for n in range(CHUNK // 128):
                top = jnp.maximum(top, s[:, 128 * n : 128 * n + 128])
            return top

        top = lax.fori_loop(lo, hi, scores, jnp.full((256, 128), -1e30, F32))
        top = jnp.max(top, axis=1, keepdims=True)

        def weights(i, carry):
            total, inner = carry
            at = pl.ds(pl.multiple_of(i * CHUNK, CHUNK), CHUNK)
            e = jnp.exp(s_buf[:, at] - top)
            s_buf[:, at] = e
            dp = dot(d_n, vt[rows, at])
            p_buf[:, at] = dp
            ep = e * dp
            for n in range(CHUNK // 128):
                total = total + e[:, 128 * n : 128 * n + 128]
                inner = inner + ep[:, 128 * n : 128 * n + 128]
            return total, inner

        zero = jnp.zeros((256, 128), F32)
        total, inner = lax.fori_loop(lo, hi, weights, (zero, zero))
        over = 1.0 / jnp.sum(total, axis=1, keepdims=True)
        inner = jnp.sum(inner, axis=1, keepdims=True) * over

        def products(i, carry):
            out, dq = carry
            at = pl.ds(pl.multiple_of(i * CHUNK, CHUNK), CHUNK)
            p = s_buf[:, at] * over
            pb = p.astype(BF)
            ds = (p * (p_buf[:, at] - inner)).astype(BF)
            out = out + dot_nt(pb, vt[rows, at])
            dq = dq + dot_nt(ds, kt[rows, at])
            dvt[rows, at] += dot(d_t, pb)
            dkt[rows, at] += dot(q_t, ds)
            return out, dq

        small = jnp.zeros((256, HD), F32)
        out, dq = lax.fori_loop(lo, hi, products, (small, small))
        oqt[tile, rows, :] = out.T
        oqt[tile, HC + HD * h : HC + HD * h + HD, :] = (dq * 0.125).T

    for tile in range(2):
        for h in range(NH):
            one_head(tile, h)

    for g in range(2):
        cols = slice(128 * g, 128 * g + 128)
        low, high = oqt[0, :, cols], oqt[1, :, cols]
        one = jnp.where(left, low, pltpu.roll(high, 64, 1))
        two = jnp.where(left, pltpu.roll(low, 64, 1), high)
        o_q[2 * g] = pltpu.roll(one, 64 * nums[64 + 2 * g], 1).astype(BF)
        o_q[2 * g + 1] = pltpu.roll(two, 64 * nums[65 + 2 * g], 1).astype(BF)

    half_left = left[:HC]

    def unsort(j, carry):
        slot0, slot1, f0, f1 = pair(j)
        at_low = pl.ds(pl.multiple_of(j * 128, 128), 128)
        at_high = pl.ds(pl.multiple_of((31 - j) * 128, 128), 128)
        for n, full in enumerate((dkt, dvt)):
            low, high = full[:, at_low], full[:, at_high]
            one = jnp.where(half_left, low, high)
            two = jnp.where(half_left, high, low)
            to = slice(n * HC, n * HC + HC)
            d_kv[slot0, to] = pltpu.roll(one, 64 * f0, 1).astype(BF)
            d_kv[slot1, to] = pltpu.roll(two, 64 * (1 - f1), 1).astype(BF)
        return carry

    lax.fori_loop(0, 16, unsort, 0)


def attention(nums, kv_all, qd_all, t_q, s_q):
    length = 32 * kv_all.shape[2]
    return pl.pallas_call(
        attention_kernel,
        out_shape=(
            jax.ShapeDtypeStruct(kv_all.shape, BF),
            jax.ShapeDtypeStruct(qd_all.shape, BF),
        ),
        in_specs=[pl.BlockSpec(memory_space=pltpu.SMEM)] + vmem(4),
        out_specs=tuple(vmem(2)),
        scratch_shapes=[
            pltpu.VMEM((HC, length), BF),
            pltpu.VMEM((HC, length), BF),
            pltpu.VMEM((HC, length), F32),
            pltpu.VMEM((HC, length), F32),
            pltpu.VMEM((2, 2 * HC, 256), F32),
            pltpu.VMEM((2, 2 * HC, 256), F32),
            pltpu.VMEM((256, length), F32),
            pltpu.VMEM((256, length), F32),
        ],
        compiler_params=pltpu.CompilerParams(vmem_limit_bytes=LIMIT),
    )(nums, kv_all, qd_all, t_q, s_q)


def back_kernel(
    d_kv, o_q, zpart, out, z_all, got, part, far, ready, sc, rc, sx, rx, sy, ry, sq, rq, sz, rz
):
    z = lax.axis_index("shard")
    c, y, x, k = spots()
    z_peer = [{"shard": lax.rem(z + d, 4)} for d in range(4)]
    half = d_kv.shape[1]
    sibling = {"ctx": c + 1 - 2 * k}
    y_peer = [{"ctx": place(lax.rem(y + d, 4), x, k)} for d in range(4)]
    x_peer = [{"ctx": place(y, lax.rem(x + d, 4), k)} for d in range(4)]
    greet(y_peer[1:] + x_peer[1:] + z_peer[1:] + [sibling])
    near = {}
    for e in (1, 3, 2, 0):
        xp = lax.rem(x + e, 4)
        near[e] = send(
            d_kv.at[pl.ds(xp * 8 + (1 - k) * 4, 4)], got.at[xp], sc.at[e], rc.at[e], sibling
        )
    tail = []
    for d in (1, 3, 2):
        yp = lax.rem(y + d, 4)
        tail.append(
            send(o_q.at[yp], out.at[y, pl.ds(half, half)], sq.at[d - 1], rq.at[d - 1], y_peer[d])
        )
    for d in (1, 3, 2):
        zp = lax.rem(z + d, 4)
        tail.append(send(zpart.at[zp], z_all.at[z], sz.at[d - 1], rz.at[d - 1], z_peer[d]))
    out[y, half:] = o_q[y]
    z_all[z] = zpart[z]
    across = {}
    for e in (1, 3, 2, 0):
        xp = lax.rem(x + e, 4)
        near[e].wait_recv()
        for n in range(4):
            both = d_kv[xp * 8 + k * 4 + n].astype(F32) + got[xp, n].astype(F32)
            part[xp, n] = both.astype(BF)
        if e:
            across[e] = send(part.at[xp], far.at[e - 1], sx.at[e - 1], rx.at[e - 1], x_peer[e])
    for e in (1, 3, 2):
        across[e].wait_recv()
    for d in (1, 3, 2, 0):
        yp = lax.rem(y + d, 4)
        total = part[x, yp].astype(F32)
        for e in range(3):
            total = total + far[e, yp].astype(F32)
        if d:
            ready[yp] = total.astype(BF)
            tail.append(
                send(ready.at[yp], out.at[y, pl.ds(0, half)], sy.at[d - 1], ry.at[d - 1], y_peer[d])
            )
        else:
            out[y, 0:half] = total.astype(BF)
    for copy in tail:
        copy.wait()
    for e in range(4):
        near[e].wait_send()
        if e:
            across[e].wait_send()


def back(d_kv, o_q, zpart):
    _, half, cols = d_kv.shape
    return pl.pallas_call(
        back_kernel,
        out_shape=(
            jax.ShapeDtypeStruct((4, 2 * half, cols), BF),
            jax.ShapeDtypeStruct(zpart.shape, BF),
        ),
        in_specs=vmem(3),
        out_specs=tuple(vmem(2)),
        scratch_shapes=[
            pltpu.VMEM((4, 4, half, cols), BF),
            pltpu.VMEM((4, 4, half, cols), BF),
            pltpu.VMEM((3, 4, half, cols), BF),
            pltpu.VMEM((4, half, cols), BF),
            dma(4), dma(4), dma(3), dma(3), dma(3), dma(3), dma(3), dma(3), dma(3), dma(3),
        ],
        compiler_params=params(2),
    )(d_kv, o_q, zpart)


def sum_kernel(
    pack, zpart, small, full, z_all, small_all,
    got, one, far_a, two, far_b, three, last, s1, s2, s3, s4,
    sz, rz, sc, rc, sa, ra, sb, rb, st, rt, gb, hb, ga, ha, gc, hc, sm, rm,
):
    z = lax.axis_index("shard")
    c, y, x, k = spots()
    sibling = {"ctx": c + 1 - 2 * k}
    z_peer = [{"shard": lax.rem(z + d, 4)} for d in range(4)]
    a = x + k * (y - x)
    b = y + k * (x - y)
    a_peer, b_peer = [], []
    for d in range(4):
        ax, by = lax.rem(a + d, 4), lax.rem(b + d, 4)
        a_peer.append({"ctx": place(b + k * (ax - b), ax + k * (b - ax), k)})
        b_peer.append({"ctx": place(by + k * (a - by), a + k * (by - a), k)})
    greet(a_peer[1:] + b_peer[1:] + z_peer[1:] + [sibling])
    near = {}
    for d in (1, 3, 2, 0):
        ap = lax.rem(b + d, 4)
        near[d] = send(pack.at[1 - k, ap], got.at[ap], sc.at[d], rc.at[d], sibling)
    tail = [send(small, s1, sm.at[0], rm.at[0], sibling)]
    for d in (1, 3, 2):
        zp = lax.rem(z + d, 4)
        tail.append(send(zpart.at[zp], z_all.at[z], sz.at[d - 1], rz.at[d - 1], z_peer[d]))
    z_all[z] = zpart[z]
    across = {}
    for d in (1, 3, 2, 0):
        ap = lax.rem(a + d, 4)
        near[d].wait_recv()
        for n in range(4):
            both = pack[k, ap, n].astype(F32) + got[ap, n].astype(F32)
            one[ap, n] = both.astype(BF)
        if d:
            across[d] = send(one.at[ap], far_a.at[d - 1], sa.at[d - 1], ra.at[d - 1], a_peer[d])
    tail[0].wait()
    s2[0] = small[...] + s1[...]
    small_a = [send(s2.at[0], s2.at[d], sm.at[d], rm.at[d], a_peer[d]) for d in (1, 2, 3)]
    for d in (1, 3, 2):
        across[d].wait_recv()
    beyond = {}
    for d in (1, 3, 2, 0):
        bp = lax.rem(b + d, 4)
        total = one[a, bp].astype(F32)
        for n in range(3):
            total = total + far_a[n, bp].astype(F32)
        two[bp] = total.astype(BF)
        if d:
            beyond[d] = send(two.at[bp], far_b.at[d - 1], sb.at[d - 1], rb.at[d - 1], b_peer[d])
    for copy in small_a:
        copy.wait()
    s3[0] = (s2[0] + s2[1]) + (s2[2] + s2[3])
    small_b = [send(s3.at[0], s3.at[d], sm.at[3 + d], rm.at[3 + d], b_peer[d]) for d in (1, 2, 3)]
    for d in (1, 3, 2):
        beyond[d].wait_recv()
    total = two[b].astype(F32)
    for n in range(3):
        total = total + far_b[n].astype(F32)
    three[...] = total.astype(BF)
    turned = []
    for d in (1, 3, 2):
        zp = lax.rem(z + d, 4)
        turned.append(
            send(
                three.at[pl.ds(2 * zp, 2)], last.at[pl.ds(2 * z, 2)],
                st.at[d - 1], rt.at[d - 1], z_peer[d],
            )
        )
    last[pl.ds(2 * z, 2)] = three[pl.ds(2 * z, 2)]
    last[8:] = three[8:]
    for copy in small_b:
        copy.wait()
    s4[...] = (s3[0] + s3[1]) + (s3[2] + s3[3])
    for d in (1, 3, 2):
        tail.append(send(s4, small_all.at[z], sm.at[6 + d], rm.at[6 + d], z_peer[d]))
    small_all[z] = s4[...]
    for copy in turned:
        copy.wait()
    full[k, a, b] = last[...]
    out_b = {}
    for d in (1, 3, 2):
        out_b[d] = send(last, full.at[k, a, b], gb.at[d - 1], hb.at[d - 1], b_peer[d])
    for d in (1, 3, 2):
        out_b[d].wait()
    out_a = {}
    for d in (1, 3, 2):
        out_a[d] = send(full.at[k, a], full.at[k, a], ga.at[d - 1], ha.at[d - 1], a_peer[d])
    tail.append(send(full.at[k, a], full.at[k, a], gc.at[0], hc.at[0], sibling))
    for d in (1, 3, 2):
        out_a[d].wait_recv()
        ap = lax.rem(a + 4 - d, 4)
        tail.append(send(full.at[k, ap], full.at[k, ap], gc.at[d], hc.at[d], sibling))
    for copy in tail[1:]:
        copy.wait()
    for d in (1, 2, 3):
        out_a[d].wait_send()
        across[d].wait_send()
        beyond[d].wait_send()
    for d in range(4):
        near[d].wait_send()


def sums(pack, zpart, small):
    tiles = pack.shape[3:]
    return pl.pallas_call(
        sum_kernel,
        out_shape=(
            jax.ShapeDtypeStruct(pack.shape, BF),
            jax.ShapeDtypeStruct(zpart.shape, BF),
            jax.ShapeDtypeStruct((4,) + small.shape, F32),
        ),
        in_specs=vmem(3),
        out_specs=tuple(vmem(3)),
        scratch_shapes=[
            pltpu.VMEM((4, 4) + tiles, BF),
            pltpu.VMEM((4, 4) + tiles, BF),
            pltpu.VMEM((3, 4) + tiles, BF),
            pltpu.VMEM((4,) + tiles, BF),
            pltpu.VMEM((3,) + tiles, BF),
            pltpu.VMEM(tiles, BF),
            pltpu.VMEM(tiles, BF),
            pltpu.VMEM(small.shape, F32),
            pltpu.VMEM((4,) + small.shape, F32),
            pltpu.VMEM((4,) + small.shape, F32),
            pltpu.VMEM(small.shape, F32),
            dma(3), dma(3), dma(4), dma(4), dma(3), dma(3), dma(3), dma(3), dma(3), dma(3),
            dma(3), dma(3), dma(3), dma(3), dma(4), dma(4), dma(10), dma(10),
        ],
        compiler_params=params(3),
    )(pack, zpart, small)


def after_kernel(ret, h_all, c_all, normed, wq, w_out, cs, given, zpart, pack, small, dj, mt):
    count = h_all.shape[1]
    for s in range(4):
        cosine, sine = cs[s, 0:8], -cs[s, 8:16]
        r = ret[s].astype(F32)
        rows = [turned(r[3 * HC + HD * h : 3 * HC + HD * h + HD], cosine, sine) for h in range(NH)]
        rows += [turned(r[HD * h : HD * h + HD], cosine, sine) for h in range(NH)]
        rows.append(r[HC : 2 * HC])
        dj[count * s : count * s + count] = jnp.concatenate(rows, axis=0).T.astype(BF)
        mt[:, count * s : count * s + count] = ret[s, 2 * HC : 3 * HC]
    cot = c_all[...].reshape(4 * count, D)
    xhat, _ = normalize(h_all[...].reshape(4 * count, D).astype(F32))
    d_one = dot_nt(dj[...], wq[...].reshape(D, 3 * HC))
    branch = dot(mt[...].astype(F32).T.astype(BF), w_out[...])
    for s in range(4):
        zpart[s, 0] = branch[count * s : count * s + count].astype(BF)
        zpart[s, 1] = d_one[count * s : count * s + count].astype(BF)
    small[...] = given[...]
    small[0:1] = jnp.sum(d_one * xhat, axis=0, keepdims=True)
    small[1:2] = jnp.sum(d_one, axis=0, keepdims=True)
    small[6:7, 0 : 3 * HC] = jnp.sum(dj[...].astype(F32), axis=0, keepdims=True)
    pack[24:32] = jnp.zeros((8,) + pack.shape[1:], BF)
    g = dot_tn(normed[...], dj[...])
    for p in range(4):
        mine = g[HC * p : HC * p + HC]
        for j in range(4):
            tiles = mine[:, 128 * j : 128 * j + 128].astype(BF).reshape(6, 2, 16, 128)
            pack[6 * j : 6 * j + 6, 2 * p : 2 * p + 2] = tiles
        rest = jnp.concatenate([mine[: HC // 2, 512:], mine[HC // 2 :, 512:]], axis=1)
        pack[24:27, 2 * p : 2 * p + 2] = rest.astype(BF).reshape(3, 2, 16, 128)
    g = dot(mt[...], cot)
    for j in range(6):
        tiles = g[:, 128 * j : 128 * j + 128].astype(BF).reshape(4, 3, 16, 128)
        pack[4 * j : 4 * j + 4, 8:11] = tiles


def after(ret, h_all, c_all, normed, wq, w_out, cs, given):
    count = h_all.shape[1]
    return pl.pallas_call(
        after_kernel,
        out_shape=(
            jax.ShapeDtypeStruct((4, 2, count, D), BF),
            jax.ShapeDtypeStruct((32, 11, 16, 128), BF),
            jax.ShapeDtypeStruct((8, D), F32),
        ),
        in_specs=vmem(8),
        out_specs=tuple(vmem(3)),
        scratch_shapes=[pltpu.VMEM((4 * count, 3 * HC), BF), pltpu.VMEM((HC, 4 * count), BF)],
        compiler_params=pltpu.CompilerParams(vmem_limit_bytes=LIMIT),
    )(ret, h_all, c_all, normed, wq, w_out, cs, given)


def finish_kernel(hid, cot, z_one, z_two, s_all, full, small_all, out, grad, g_qkv, g_out, vecs):
    z = lax.axis_index("shard")
    branch, d_one, d_two = 0.0, 0.0, 0.0
    for p in range(4):
        branch = branch + (z_one[p, 0].astype(F32) + z_two[p, 0].astype(F32))
        d_one = d_one + z_one[p, 1].astype(F32)
        d_two = d_two + z_two[p, 1].astype(F32)
    flat = hid[...].astype(F32)
    xhat, r = normalize(flat)
    out[...] = (flat + branch + vector(s_all, 4) + vector(s_all, 5)).astype(BF)
    g = d_one * vector(s_all, 0) + d_two * vector(s_all, 2)
    inner = jnp.mean(g * xhat, axis=-1, keepdims=True)
    grad[...] = cot[...].astype(F32) + r * (g - jnp.mean(g, axis=-1, keepdims=True) - xhat * inner)
    planes = []
    for p in range(4):
        cols = [full[6 * j : 6 * j + 6, 2 * p : 2 * p + 2].reshape(HC, 128) for j in range(4)]
        rest = full[24:27, 2 * p : 2 * p + 2].reshape(HC // 2, 128).astype(F32)
        rest = jnp.concatenate([rest[:, :64], rest[:, 64:]], axis=0)
        planes.append(jnp.concatenate([col.astype(F32) for col in cols] + [rest], axis=1))
    for t in range(3):
        g_qkv[:, D * t : D * t + D] = jnp.concatenate(
            [plane[:, HC * t : HC * t + HC] for plane in planes], axis=1
        )
    for j in range(6):
        tiles = full[4 * j : 4 * j + 4, 8:11].reshape(HC, 128)
        g_out[:, 128 * j : 128 * j + 128] = tiles.astype(F32)
    total = (small_all[0] + small_all[1]) + (small_all[2] + small_all[3])
    own = small_all[z]
    rows = jnp.concatenate([total[0:4], own[4:5]], axis=0)
    piece = jnp.zeros((5, HC), F32)
    for p in range(4):
        piece = piece + jnp.where(z == p, rows[:, HC * p : HC * p + HC], 0.0)
    vecs[...] = jnp.zeros_like(vecs)
    vecs[0:5] = piece
    for i in range(3):
        piece = jnp.zeros((1, HC), F32)
        for p in range(4):
            n = 3 * p + i
            at = HC * (n // 4)
            piece = piece + jnp.where(z == p, small_all[n % 4, 6:7, at : at + HC], 0.0)
        vecs[8 + i : 9 + i] = piece
    for i in range(4):
        vecs[11 + i : 12 + i] = own[5:6, HC * i : HC * i + HC]


def finish(hid, cot, z_one, z_two, s_all, full, small_all):
    return pl.pallas_call(
        finish_kernel,
        out_shape=(
            jax.ShapeDtypeStruct(hid.shape, BF),
            jax.ShapeDtypeStruct(hid.shape, F32),
            jax.ShapeDtypeStruct((HC, 3 * D), F32),
            jax.ShapeDtypeStruct((HC, D), F32),
            jax.ShapeDtypeStruct((16, HC), F32),
        ),
        in_specs=vmem(7),
        out_specs=tuple(vmem(5)),
        compiler_params=pltpu.CompilerParams(vmem_limit_bytes=LIMIT),
    )(hid, cot, z_one, z_two, s_all, full, small_all)


def local(
    hidden, ln1_gain, ln1_bias, ln2_gain, ln2_bias, w_qkv, b_qkv, w_out, b_out, w_up, b_up,
    w_down, b_down, block_order, positions, cotangent,
):
    rows = hidden.shape[0]
    c, y, x, k = spots()
    vectors = [v.reshape(1, HC) for v in (ln1_gain, ln1_bias, ln2_gain, ln2_bias, b_out, b_down)]
    vectors.append(b_qkv.reshape(3, HC))
    meta = jnp.concatenate(
        [positions.reshape(32, 128), jnp.pad(block_order, ((0, 7), (0, 64)))], axis=0
    )
    h_all, c_all, wq, wu, s_all, m_all = spread(hidden, cotangent, w_qkv, w_up, vectors, meta)

    places = m_all[:, :32].reshape(4, 64, 64)
    order = m_all[:, 32, :64]
    blocks = jnp.arange(64, dtype=jnp.int32)

    def pick(table, which):
        hit = which[..., None] == blocks
        return jnp.sum(jnp.where(hit[..., None], table, 0), axis=-2)

    mine = lax.dynamic_slice(order, (0, 2 * c), (4, 2))
    pos = pick(places[:, None], mine).reshape(4, 1, rows)
    freqs = jnp.power(10000.0, -jnp.arange(0, ROT, 2, dtype=F32) / ROT)
    angle = pos.astype(F32) * freqs[:, None]
    cs = jnp.concatenate([jnp.cos(angle), jnp.sin(angle)], axis=1)

    order_y = lax.dynamic_index_in_dim(order, y, axis=0, keepdims=False)
    places_y = lax.dynamic_index_in_dim(places, y, axis=0, keepdims=False)
    first = order_y.reshape(32, 2)[:, 0]
    flip = (first >= 32).astype(jnp.int32)
    low = jnp.minimum(first, 63 - first)
    slots = jnp.asarray([((i // 2) % 4) * 8 + (i % 2) * 4 + i // 8 for i in range(32)], jnp.int32)
    hit = low[None, :] == jnp.arange(32, dtype=jnp.int32)[:, None]
    slot_of = jnp.sum(jnp.where(hit, slots[None], 0), axis=1)
    flip_of = jnp.sum(jnp.where(hit, flip[None], 0), axis=1)
    low_q = lax.dynamic_index_in_dim(low.reshape(4, 8), x * 2 + k, axis=1, keepdims=False)
    flip_q = lax.dynamic_index_in_dim(flip.reshape(4, 8), x * 2 + k, axis=1, keepdims=False)
    block_q = jnp.stack([low_q, 63 - low_q])
    t_q = block_q[..., None] * 64 + blocks
    s_q = t_q - pick(places_y, block_q)
    reach = jnp.stack(
        [jnp.min(s_q, axis=(1, 2)) // CHUNK, jnp.max(t_q, axis=(1, 2)) // CHUNK + 1], axis=1
    )
    nums = jnp.concatenate([slot_of, flip_of, flip_q, reach.reshape(4)]).astype(jnp.int32)

    zpart_two, g_up, g_down, small = feed(
        h_all, c_all, wu, w_down, s_all, b_up.astype(F32).reshape(1, -1)
    )
    qkvd, normed = project(h_all, c_all, wq, s_all, cs, w_out)
    kv_all, qd_all, u_all = gather(qkvd, g_up)
    u_sum, down_sum = lax.psum((u_all, g_down), "ctx")
    d_kv, o_q = attention(nums, kv_all, qd_all, t_q.reshape(2, 256, 1), s_q.reshape(2, 256, 1))
    returned, z_two = back(d_kv, o_q, zpart_two)
    zpart_one, pack, small = after(returned, h_all, c_all, normed, wq, w_out, cs, small)
    full, z_one, small_all = sums(pack.reshape(2, 4, 4, 11, 16, 128), zpart_one, small)
    output, grad_input, grad_w_qkv, grad_w_out, vecs = finish(
        hidden, cotangent, z_one, z_two, s_all, full.reshape(32, 11, 16, 128), small_all
    )
    grad_w_up = u_sum.swapaxes(0, 1).reshape(w_up.shape).astype(F32)
    grad_w_down = down_sum.astype(F32)
    return (
        output, grad_input, vecs[0], vecs[1], vecs[2], vecs[3],
        grad_w_qkv, vecs[8:11].reshape(-1), grad_w_out, vecs[4], grad_w_up,
        vecs[11:15].reshape(-1), grad_w_down, vecs[4],
    )


def solution(mesh):
    tokens, vector, matrix = P(("shard", "ctx"), None), P("shard"), P("shard", None)
    return jax.shard_map(
        local,
        mesh=mesh,
        in_specs=(
            tokens, vector, vector, vector, vector, matrix, vector, matrix, vector, matrix, vector,
            matrix, vector, matrix, matrix, tokens,
        ),
        out_specs=(
            tokens, tokens, vector, vector, vector, vector, matrix, vector, matrix, vector, matrix,
            vector, matrix, vector,
        ),
        check_vma=False,
    )
```

time: 888 us -> 246 us (0.28)
  waiting for transfers between devices: 437 us -> 0.03 us
  Pallas kernels: 0 us -> 202 us
  matrix products: 190 us -> 0 us
  blocking collectives: 105 us -> 0 us
  local copies, waits for them, and re-layouts: 108 us -> 19.7 us
  other arithmetic: 27.1 us -> 9.08 us
    pallas_call x0 -> x9, Pallas kernels: none -> 202 us  [the longest x1 41.8 us: attention(): pl.pallas_call(attention_kernel, out_shape=(jax.ShapeDtypeStruct(kv_all.s...]
    dot_general x54 -> x0, matrix products: 190 us -> none  [the longest x6 43.9 us: backward_group(): jnp.einsum('hrk,rhd->khd', d_scores, query_heads, preferred_element_type=...]
    reduce_scatter x4 -> x0, waiting for transfers between devices: 165 us -> none  [the longest x1 53.2 us: local(): lax.psum_scatter(grads[10].astype(jnp.bfloat16), 'shard', scatter_dimensi...]
    unnamed x15 -> x1, waiting for transfers between devices: 132 us -> 0.02 us
    all_gather x6 -> x0, waiting for transfers between devices: 115 us -> none  [the longest x1 47.2 us: local(): lax.all_gather(key_b, 'ctx', axis=0, tiled=True)]
    psum x1 -> x0, blocking collectives: 67.5 us -> none  [local(): lax.psum(partial_sums[0].astype(jnp.bfloat16), 'ctx').astype(jnp.float32)]
    dynamic_slice x36 -> x4, local copies, waits for them, and re-layouts: 30.7 us -> 0.46 us  [the longest x1 0.19 us: local(): lax.dynamic_index_in_dim(low.reshape(4, 8), x * 2 + k, axis=1, keepdims=F...]
    unnamed x64 -> x9, local copies, waits for them, and re-layouts: 28.1 us -> 0.58 us
  transfers between devices with their start and end apart: 13 -> 1, of which waited for: 10 -> 0; matrix products, arithmetic and copies ran while one was open for 36% -> 3% of each run, Pallas kernels for 0% -> 52%
where the time goes in v1:
time: 246 us; the launch traced here: 245 us
  Pallas kernels  202 us (82%)
  local copies, waits for them, and re-layouts  19.7 us (8%)
  between operations  14.3 us (6%)
  other arithmetic  9.08 us (4%)
    pallas_call x1, Pallas kernels, attention(): pl.pallas_call(attention_kernel, out_shape=(jax.ShapeDtypeStruct(kv_all.s...  41.8 us
    pallas_call x1, Pallas kernels, sums(): pl.pallas_call(sum_kernel, out_shape=(jax.ShapeDtypeStruct(pack.shape, BF...  40.5 us
    pallas_call x1, Pallas kernels, spread(): pl.pallas_call(spread_kernel, out_shape=(jax.ShapeDtypeStruct((4, rows, D...  36 us
    pallas_call x1, Pallas kernels, back(): pl.pallas_call(back_kernel, out_shape=(jax.ShapeDtypeStruct((4, 2 * half,...  34.9 us
    pallas_call x1, Pallas kernels, gather(): pl.pallas_call(gather_kernel, out_shape=(jax.ShapeDtypeStruct((32, rows /...  26.7 us
    pallas_call x1, Pallas kernels, feed(): pl.pallas_call(feed_kernel, out_shape=(jax.ShapeDtypeStruct((4, 2, count,...  7.67 us
    reshape x6, local copies, waits for them, and re-layouts, local(): v.reshape(1, HC)  7.32 us
    pallas_call x1, Pallas kernels, after(): pl.pallas_call(after_kernel, out_shape=(jax.ShapeDtypeStruct((4, 2, count...  5.52 us
  transfers between devices with their start and end apart: 1, of which 0 were waited for; matrix products, arithmetic and copies ran while one was open for 3% of the time, Pallas kernels for 52%

profile of v1, /device:TPU:1, one launch (start us, length us, event | category | flops | bytes accessed | tf_op | source)
XLA Modules:
  0.0 245.2 jit_solution(12850704019593882417)
XLA Ops:
  7.2 0.0 copy-start.2
  7.2 0.0 all-reduce.4.cloned.1.call-start
  7.3 1.2 reshape.334.g1
  8.5 1.2 reshape.335.b1
  9.7 1.2 reshape.336.g2
  10.9 1.2 reshape.337.b2
  12.1 1.2 reshape.338.bo
  13.4 1.2 reshape.339.bd
  14.6 1.3 reshape.340.bq
  15.9 1.3 pad_add_fusion.meta
  17.3 36.0 %shard_map.272 = (bf16[4,128,768]{2,1,0:T(8,128)(2,1)}, bf16[4,128,768]{2,1,0:T(8,128)(2,1)}, bf16[4,192,576]{2,1,0:T(8,128)(2,1)}, bf16[4,192,768]{2,1,0:T(8,12...) custom-call(bf16[128,768]{1,0:T(8,128)(2,1)} %hid.3, bf16[128,768]{1,0:T(8,128)(2,1)} %cot.3, ...), custom_call_target="tpu_custom_call" | custom-call | tf_op jit(solution)/shard_map/pallas_call | solution.py:148
  53.3 0.7 slice.31
  54.0 0.8 slice.33
  54.8 0.0 copy-done.2
  54.8 0.6 reshape.352.b_up
  55.4 0.1 constant_dynamic-slice_fusion
  55.5 0.1 iota_compare_fusion.1
  55.6 0.1 reshape.343
  55.6 0.1 select_reduce_fusion
  55.8 0.1 convert_element_type.37
  55.9 0.1 multiply_cosine_fusion
  56.0 0.6 pad_maximum_fusion.cs
  56.7 4.1 %shard_map.273 = (bf16[4,768,128]{2,1,0:T(8,128)(2,1)}, bf16[512,768]{1,0:T(8,128)(2,1)}) custom-call(bf16[4,128,768]{2,1,0:T(8,128)(2,1)} %get-tuple-element.45.h_all, bf16[4,128,768]{2,1,0:T(8,128)(2,1)} %get-tuple-element.46.c_all, bf16[4,192,576]{2,1,0:T(8,128)(2,1)} %get-tuple-element.47.wq, f32[4,16,192]{2,1,0:T(8,128)} %get-tuple-element.48.s_all, ...), custom_call_target="tpu_custom_call" | custom-call | tf_op jit(solution)/shard_map/pallas_call | solution.py:227
  60.8 7.7 %shard_map.274 = (bf16[4,2,128,768]{3,2,1,0:T(8,128)(2,1)}, bf16[4,192,768]{2,1,0:T(8,128)(2,1)}, bf16[768,768]{1,0:T(8,128)(2,1)}, f32[8,768]{1,0:T(8,128)}) custom-call(bf16[4,128,768]{2,1,0:T(8,128)(2,1)} %get-tuple-element.45.h_all, bf16[4,128,768]{2,1,0:T(8,128)(2,1)} %get-tuple-element.46.c_all, bf16[4,192,768]{2,1,0:T(8,128)(2,1)} %get-tuple-element.50.wu, ...), custom_call_target="tpu_custom_call" | custom-call | tf_op jit(solution)/shard_map/pallas_call | solution.py:266
  68.5 26.7 %shard_map.275 = (bf16[32,384,128]{2,1,0:T(8,128)(2,1)}, bf16[4,384,128]{2,1,0:T(8,128)(2,1)}, bf16[4,192,768]{2,1,0:T(8,128)(2,1)}) custom-call(bf16[4,768,128]{2,1,0:T(8,128)(2,1)} %get-tuple-element.49.qkvd, bf16[4,192,768]{2,1,0:T(8,128)(2,1)} %get-tuple-element.51.g_up), custom_call_target="tpu_custom_call" | custom-call | tf_op jit(solution)/shard_map/pallas_call | solution.py:345
  95.2 2.4 copy.54
  97.6 0.0 copy-start.3
  97.6 0.0 all-reduce.4.cloned.1.call-update
  97.7 0.1 reshape.342
  97.8 0.1 slice_reduce_fusion
  97.9 0.1 squeeze.34
  98.1 0.2 dynamic-slice_reduce_fusion
  98.3 0.1 iota_compare_fusion.2
  98.3 0.2 select_reduce_fusion.1
  98.5 0.2 subtract_reduce_fusion
  98.8 0.2 reduce_sum.43
  99.0 0.1 add.97
  99.1 0.2 dynamic-slice_reduce_fusion.1
  99.3 0.1 copy.46
  99.4 0.1 reshape.344
  99.4 0.1 add.89
  99.5 0.2 add.100
  99.8 0.0 copy-done.3
  99.8 0.1 select_reduce_fusion.3
  99.9 0.6 pad_add_fusion.3.nums
  100.5 0.9 fusion.3
  101.4 41.8 %shard_map.276 = (bf16[32,384,128]{2,1,0:T(8,128)(2,1)}, bf16[4,384,128]{2,1,0:T(8,128)(2,1)}) custom-call(s32[72]{0:T(128)} %pad_add_fusion.3.nums, bf16[32,384,128]{2,1,0:T(8,128)(2,1)} %get-tuple-element.52.kv_all, bf16[4,384,128]{2,1,0:T(8,128)(2,1)} %get-tuple-element.53.qd_all, s32[2,256,1]{2,1,0:T(8,128)} %get-tuple-element.81.t_q, ...), custom_call_target="tpu_custom_call" | custom-call | tf_op jit(solution)/shard_map/pallas_call | solution.py:488
  143.2 34.9 %shard_map.277 = (bf16[4,768,128]{2,1,0:T(8,128)(2,1)}, bf16[4,2,128,768]{3,2,1,0:T(8,128)(2,1)}) custom-call(bf16[32,384,128]{2,1,0:T(8,128)(2,1)} %get-tuple-element.54.d_kv, bf16[4,384,128]{2,1,0:T(8,128)(2,1)} %get-tuple-element.55.o_q, bf16[4,2,128,768]{3,2,1,0:T(8,128)(2,1)} %get-tuple-element.56.zpart), custom_call_target="tpu_custom_call" | custom-call | tf_op jit(solution)/shard_map/pallas_call | solution.py:571
  178.0 5.5 %shard_map.278 = (bf16[4,2,128,768]{3,2,1,0:T(8,128)(2,1)}, bf16[32,11,16,128]{3,2,1,0:T(8,128)(2,1)}, f32[8,768]{1,0:T(8,128)}) custom-call(bf16[4,768,128]{2,1,0:T(8,128)(2,1)} %get-tuple-element.57.ret, bf16[4,128,768]{2,1,0:T(8,128)(2,1)} %get-tuple-element.45.h_all, bf16[4,128,768]{2,1,0:T(8,128)(2,1)} %get-tuple-element.46.c_all, ...), custom_call_target="tpu_custom_call" | custom-call | tf_op jit(solution)/shard_map/pallas_call | solution.py:760
  183.5 40.5 %shard_map.279 = (bf16[2,4,4,11,16,128]{5,4,3,2,1,0:T(8,128)(2,1)}, bf16[4,2,128,768]{3,2,1,0:T(8,128)(2,1)}, f32[4,8,768]{2,1,0:T(8,128)}) custom-call(bf16[2,4,4,11,16,128]{5,4,3,2,1,0:T(8,128)(2,1)} %bitcast.35, bf16[4,2,128,768]{3,2,1,0:T(8,128)(2,1)} %get-tuple-element.61.zpart, f32[8,768]{1,0:T(8,128)} %get-tuple-element.62.small), custom_call_target="tpu_custom_call" | custom-call | tf_op jit(solution)/shard_map/pallas_call | solution.py:694
  224.0 4.9 %shard_map.280 = (bf16[128,768]{1,0:T(8,128)(2,1)}, f32[128,768]{1,0:T(8,128)}, f32[192,2304]{1,0:T(8,128)}, f32[192,768]{1,0:T(8,128)}, f32[16,192]{1,0:T(8,128)}) custom-call(bf16[128,768]{1,0:T(8,128)(2,1)} %hid.3, bf16[128,768]{1,0:T(8,128)(2,1)} %cot.3, bf16[4,2,128,768]{3,2,1,0:T(8,128)(2,1)} %get-tuple-element.63.z_one, ...), custom_call_target="tpu_custom_call" | custom-call | tf_op jit(solution)/shard_map/pallas_call | solution.py:820
  228.9 0.7 slice.38
  229.6 0.7 slice.40
  230.3 0.7 reshape.349
  231.0 0.7 reshape.350
  231.7 1.5 fusion.4
  233.1 0.0 copy-start.1
  233.1 0.0 all-reduce.4.cloned.1.call-done
  233.2 0.0 copy-start
  233.2 3.0 %convert_element_type.40 = f32[192,3072]{1,0:T(8,128)} convert(bf16[192,3072]{1,0:T(8,128)(2,1)} %get-tuple-element.78) | non-fusion elementwise | flops 589824 | bytes 3538944 | tf_op jit(solution)/shard_map/convert_element_type | solution.py:894
  236.2 0.0 copy-done
  236.2 1.6 convert_element_type.41
  237.8 0.0 copy-done.1
  237.8 0.6 copy.58
  (13 shorter events, 0.1 us)
Async XLA Ops:
  7.2 47.7 %copy-start.2 = (bf16[768]{0:T(1024)(128)(2,1)S(1)}, bf16[768]{0:T(1024)(128)(2,1)}, u32[]{:S(2)}) copy-start(bf16[768]{0:T(1024)(128)(2,1)} %param.27) | copy-start | bytes 4612
  7.2 226.0 %all-reduce.4.cloned.1.call-start = ((), (), s32[]{:S(2)}) async-start(), calls=%async_computation | async-start | bytes 4718592 | tf_op jit(solution)/shard_map/psum | solution.py:886
  97.6 2.1 copy-start.3
  233.1 4.6 %copy-start.1 = (f32[1,192]{1,0:T(1,128)}, f32[1,192]{1,0:T(1,128)S(1)}, u32[]{:S(2)}) copy-start(f32[1,192]{1,0:T(1,128)S(1)} %get-tuple-element.82) | copy-start | bytes 2308
  233.2 3.0 %copy-start = (bf16[768,768]{1,0:T(8,128)(2,1)S(1)}, bf16[768,768]{1,0:T(8,128)(2,1)}, u32[]{:S(2)}) copy-start(bf16[768,768]{1,0:T(8,128)(2,1)} %get-tuple-element.79) | copy-start | bytes 3538948
Sparse Core Ops, SparseCore 0:
  97.8 110.3 all-reduce.3

commit v2 on v1

v2 whole, which is shorter than its diff:
```python
import functools
import math

import jax
import jax.numpy as jnp
import numpy as np
from jax import lax
from jax.experimental import pallas as pl
from jax.experimental.pallas import tpu as pltpu
from jax.sharding import PartitionSpec as P

HD = 64
ROT = 16
D = 768
NH = 3
HC = NH * HD
CHUNK = 2048
MESH = pl.DeviceIdType.MESH
BF = jnp.bfloat16
F32 = jnp.float32
LIMIT = 56 * 1024 * 1024


def vmem(count):
    return [pl.BlockSpec(memory_space=pltpu.VMEM)] * count


def spots():
    c = lax.axis_index("ctx")
    return c, lax.div(c, 8), lax.rem(lax.div(c, 2), 4), lax.rem(c, 2)


def place(y, x, k):
    return y * 8 + x * 2 + k


def send(src, dst, send_sem, recv_sem, where):
    copy = pltpu.make_async_remote_copy(
        src_ref=src,
        dst_ref=dst,
        send_sem=send_sem,
        recv_sem=recv_sem,
        device_id=where,
        device_id_type=MESH,
    )
    copy.start()
    return copy


def greet(peers):
    barrier = pltpu.get_barrier_semaphore()
    for peer in peers:
        pl.semaphore_signal(barrier, inc=1, device_id=peer, device_id_type=MESH)
    pl.semaphore_wait(barrier, len(peers))


def dma(*dims):
    return pltpu.SemaphoreType.DMA(dims)


def params(ident):
    return pltpu.CompilerParams(
        collective_id=ident, has_side_effects=True, vmem_limit_bytes=LIMIT
    )


def spread_kernel(
    hid, cot, w_qkv, wu, g1, b1, g2, b2, bo, bd, bq, pos, place_of,
    h_all, c_all, wq_all, wu_all, s_all, p_all, o_all,
    wq, small, so, ro, sp, rp, sf, rf, ss, rs,
):
    z = lax.axis_index("shard")
    c, y, x, k = spots()
    sibling = {"ctx": c + 1 - 2 * k}
    peers = [{"shard": lax.rem(z + d, 4)} for d in range(4)]
    greet(peers[1:] + [sibling])
    rows = wu.shape[0]
    half = rows // 2
    width = wu_all.shape[2]
    for p in range(4):
        wq[p] = jnp.concatenate(
            [w_qkv[:, D * t + HC * p : D * t + HC * p + HC] for t in range(3)], axis=1
        )
    small[...] = jnp.zeros_like(small)
    for i, ref in enumerate((g1, b1, g2, b2, bo, bd)):
        small[i : i + 1] = ref[...].astype(F32).reshape(1, HC)
    bias = bq[...].astype(F32).reshape(1, 3 * HC)
    for i in range(3):
        small[6 + i : 7 + i] = bias[:, HC * i : HC * i + HC]

    mine = pl.ds(pl.multiple_of(k * half, 16), half)
    weights, others = {}, []
    for d in (1, 3, 2):
        p = lax.rem(z + d, 4)
        cols = pl.ds(pl.multiple_of(p * width, 128), width)
        weights[d] = [
            send(wq.at[p, mine], wq_all.at[z, mine], sp.at[0, d - 1], rp.at[0, d - 1], peers[d]),
            send(wu.at[mine, cols], wu_all.at[z, mine], sp.at[1, d - 1], rp.at[1, d - 1], peers[d]),
        ]
    cut = hid.shape[0] // 2
    parts = [pl.ds(0, cut), pl.ds(cut, cut)]
    ring = {}
    for i, (src, dst) in enumerate(((hid, h_all), (cot, c_all))):
        for n in range(2):
            ring[i, 1, n] = send(
                src.at[parts[n]], dst.at[z, parts[n]], so.at[i, 0, n], ro.at[i, 0, n], peers[1]
            )
            m = 1 - n
            ring[i, 3, m] = send(
                src.at[parts[m]], dst.at[z, parts[m]], so.at[i, 1, m], ro.at[i, 1, m], peers[3]
            )
    for d in (1, 2, 3):
        for i, (src, dst) in enumerate(((small, s_all), (pos, p_all), (place_of, o_all))):
            others.append(send(src, dst.at[z], ss.at[i, d - 1], rs.at[i, d - 1], peers[d]))
    h_all[z] = hid[...]
    c_all[z] = cot[...]
    s_all[z] = small[...]
    p_all[z] = pos[...]
    o_all[z] = place_of[...]
    wq_all[z] = wq[z]
    wu_all[z] = wu[:, pl.ds(pl.multiple_of(z * width, 128), width)]
    before, after = lax.rem(z + 3, 4), lax.rem(z + 1, 4)
    for d in (1, 3, 2):
        source = lax.rem(z + 4 - d, 4)
        for i, full in enumerate((wq_all, wu_all)):
            weights[d][i].wait_recv()
            part = full.at[source, mine]
            others.append(send(part, part, sf.at[i, d - 1], rf.at[i, d - 1], sibling))
    for i, full in enumerate((h_all, c_all)):
        ring[i, 1, 0].wait_recv()
        part = full.at[before, parts[0]]
        others.append(send(part, part, ss.at[3 + i, 0], rs.at[3 + i, 0], peers[1]))
        ring[i, 3, 1].wait_recv()
        part = full.at[after, parts[1]]
        others.append(send(part, part, ss.at[3 + i, 1], rs.at[3 + i, 1], peers[3]))
    for i in range(2):
        ring[i, 1, 1].wait_recv()
        ring[i, 3, 0].wait_recv()
    for copy in others:
        copy.wait()
    for d in (1, 3, 2):
        for copy in weights[d]:
            copy.wait_send()
    for copy in ring.values():
        copy.wait_send()


def spread(hid, cot, w_qkv, wu, vectors, pos, place_of):
    rows = hid.shape[0]
    width = wu.shape[1] // 4
    return pl.pallas_call(
        spread_kernel,
        out_shape=(
            jax.ShapeDtypeStruct((4, rows, D), BF),
            jax.ShapeDtypeStruct((4, rows, D), BF),
            jax.ShapeDtypeStruct((4, wu.shape[0], 3 * HC), BF),
            jax.ShapeDtypeStruct((4, wu.shape[0], width), BF),
            jax.ShapeDtypeStruct((4, 16, HC), F32),
            jax.ShapeDtypeStruct((4,) + pos.shape, jnp.int32),
            jax.ShapeDtypeStruct((4,) + place_of.shape, jnp.int32),
        ),
        in_specs=vmem(13),
        out_specs=tuple(vmem(7)),
        scratch_shapes=[
            pltpu.VMEM((4, wu.shape[0], 3 * HC), BF),
            pltpu.VMEM((16, HC), F32),
            dma(2, 2, 2), dma(2, 2, 2), dma(2, 3), dma(2, 3), dma(2, 3), dma(2, 3),
            dma(5, 3), dma(5, 3),
        ],
        compiler_params=params(0),
    )(hid, cot, w_qkv, wu, *vectors, pos, place_of)


def dot(left, right):
    return jnp.dot(left, right, preferred_element_type=F32)


def dot_nt(left, right):
    return lax.dot_general(left, right, (((1,), (1,)), ((), ())), preferred_element_type=F32)


def dot_tn(left, right):
    return lax.dot_general(left, right, (((0,), (0,)), ((), ())), preferred_element_type=F32)


def normalize(flat):
    center = flat - jnp.mean(flat, axis=-1, keepdims=True)
    r = lax.rsqrt(jnp.mean(center * center, axis=-1, keepdims=True) + 1e-05)
    return center * r, r


def vector(s_all, i):
    return jnp.concatenate([s_all[p, i : i + 1] for p in range(4)], axis=1)


def swap(v, flag):
    return jnp.where(flag > 0, pltpu.roll(v, 64, 1), v)


def turned(v, cosine, sine):
    first, second = v[0:8], v[8:16]
    return jnp.concatenate(
        [first * cosine - second * sine, second * cosine + first * sine, v[16:]], axis=0
    )


def project_kernel(flips, h_all, c_all, wq, s_all, cs, w_out, qkvd, normed):
    z = lax.axis_index("shard")
    count = h_all.shape[1]
    xhat, _ = normalize(h_all[...].reshape(4 * count, D).astype(F32))
    n1 = (xhat * vector(s_all, 0) + vector(s_all, 1)).astype(BF)
    normed[...] = n1
    bias = []
    for t in range(3):
        piece = jnp.zeros((1, HC), F32)
        for p in range(4):
            n = 4 * t + p
            piece = piece + jnp.where(z == p, s_all[n // 3, 6 + n % 3 : 7 + n % 3], 0.0)
        bias.append(piece)
    joined = dot(n1, wq[...].reshape(D, 3 * HC)) + jnp.concatenate(bias, axis=1)
    d_mixed = dot_nt(w_out[...], c_all[...].reshape(4 * count, D))
    for s in range(4):
        jt = joined[count * s : count * s + count].T
        cosine, sine = cs[s, 0:8], cs[s, 8:16]
        for h in range(NH):
            at = HD * h
            rows = [
                turned(jt[HC + at : HC + at + HD], cosine, sine),
                jt[2 * HC + at : 2 * HC + at + HD],
                turned(jt[at : at + HD], cosine, sine),
                d_mixed[at : at + HD, count * s : count * s + count],
            ]
            qkvd[s, h] = swap(jnp.concatenate(rows, axis=0), flips[s]).astype(BF)


def project(flips, h_all, c_all, wq, s_all, cs, w_out):
    count = h_all.shape[1]
    return pl.pallas_call(
        project_kernel,
        out_shape=(
            jax.ShapeDtypeStruct((4, NH, 4 * HD, count), BF),
            jax.ShapeDtypeStruct((4 * count, D), BF),
        ),
        in_specs=[pl.BlockSpec(memory_space=pltpu.SMEM)] + vmem(6),
        out_specs=tuple(vmem(2)),
        compiler_params=pltpu.CompilerParams(vmem_limit_bytes=LIMIT),
    )(flips, h_all, c_all, wq, s_all, cs, w_out)


def feed_kernel(h_all, c_all, wu, w_down, s_all, b_up, zpart, g_up, g_down, small):
    count = h_all.shape[1]
    xhat, _ = normalize(h_all[...].reshape(4 * count, D).astype(F32))
    n2 = (xhat * vector(s_all, 2) + vector(s_all, 3)).astype(BF)
    up = wu[...].reshape(D, wu.shape[2])
    cot = c_all[...].reshape(4 * count, D)
    hidden = dot(n2, up) + b_up[...]
    rise = 0.5 * (1.0 + lax.erf(hidden * (1.0 / math.sqrt(2.0))))
    slope = rise + hidden * jnp.exp(-0.5 * hidden * hidden) * (1.0 / math.sqrt(2.0 * math.pi))
    active = (hidden * rise).astype(BF)
    d_up_f = (dot_nt(cot, w_down[...]) * slope).astype(BF)
    g_down[...] = dot_tn(active, cot).astype(BF)
    g_up[...] = dot_tn(n2, d_up_f).astype(BF).reshape(g_up.shape)
    branch = dot(active, w_down[...]).astype(BF)
    d_two = dot_nt(d_up_f, up)
    for s in range(4):
        zpart[s, 0] = branch[count * s : count * s + count]
        zpart[s, 1] = d_two[count * s : count * s + count].astype(BF)
    small[...] = jnp.zeros_like(small)
    small[2:3] = jnp.sum(d_two * xhat, axis=0, keepdims=True)
    small[3:4] = jnp.sum(d_two, axis=0, keepdims=True)
    small[4:5] = jnp.sum(cot.astype(F32), axis=0, keepdims=True)
    small[5:6] = jnp.sum(d_up_f.astype(F32), axis=0, keepdims=True)


def feed(h_all, c_all, wu, w_down, s_all, b_up):
    count = h_all.shape[1]
    return pl.pallas_call(
        feed_kernel,
        out_shape=(
            jax.ShapeDtypeStruct((4, 2, count, D), BF),
            jax.ShapeDtypeStruct(wu.shape, BF),
            jax.ShapeDtypeStruct(w_down.shape, BF),
            jax.ShapeDtypeStruct((8, D), F32),
        ),
        in_specs=vmem(6),
        out_specs=tuple(vmem(4)),
        compiler_params=pltpu.CompilerParams(vmem_limit_bytes=LIMIT),
    )(h_all, c_all, wu, w_down, s_all, b_up)


def attend_kernel(
    qkvd, t_k, t_q, s_q, zpart, out, z_all,
    kv0, kv1, kv2, qd, kt, dkv, qdt, oqt, s_buf, p_buf, dpart, oq, got, part, far, ready,
    s_y, r_y, s_q1, r_q1, s_x, r_x, s_r, r_r, s_f, r_f, s_n, r_n, s_a, r_a, s_b, r_b, s_o, r_o, s_z, r_z,
):
    z = lax.axis_index("shard")
    c, y, x, k = spots()
    kvs = (kv0, kv1, kv2)
    base = x * 8 + k * 4
    sibling = {"ctx": c + 1 - 2 * k}
    y_peer = [{"ctx": place(lax.rem(y + d, 4), x, k)} for d in range(4)]
    x_peer = [{"ctx": place(y, lax.rem(x + d, 4), k)} for d in range(4)]
    z_peer = [{"shard": lax.rem(z + d, 4)} for d in range(4)]
    greet(y_peer[1:] + x_peer[1:] + z_peer[1:] + [sibling])
    tail, first, across, relay, here = [], {}, {}, {}, {0: [], 1: [], 2: []}
    order = (0, 1, 3, 2)
    for h in range(NH):
        for d in order[1:]:
            yp = lax.rem(y + d, 4)
            first[h, d] = send(
                qkvd.at[yp, h, pl.ds(0, 128)], kvs[h].at[base + y],
                s_y.at[h, d - 1], r_y.at[h, d - 1], y_peer[d],
            )
            if h == 0:
                here[0].append(
                    send(
                        qkvd.at[yp, :, pl.ds(128, 128)], qd.at[y],
                        s_q1.at[d - 1], r_q1.at[d - 1], y_peer[d],
                    )
                )
        kvs[h][base + y] = qkvd[y, h, 0:128]
    qd[y] = qkvd[y, :, 128:]
    z_all[z] = zpart[z]

    def blocks_out(h):
        for d in order:
            if d:
                first[h, d].wait_recv()
            block = kvs[h].at[base + lax.rem(y + 4 - d, 4)]
            for e in (1, 3):
                across[h, d, e] = send(
                    block, block, s_x.at[h, d, e - 1], r_x.at[h, d, e - 1], x_peer[e]
                )
            here[h].append(send(block, block, s_f.at[h, d, 1], r_f.at[h, d, 1], sibling))

    def blocks_on(h):
        for d in order:
            ys = lax.rem(y + 4 - d, 4)
            for e in (1, 3):
                across[h, d, e].wait_recv()
                block = kvs[h].at[lax.rem(x + 4 - e, 4) * 8 + k * 4 + ys]
                if e == (1, 1, 3, 3)[d]:
                    relay[h, d] = send(block, block, s_r.at[h, d], r_r.at[h, d], x_peer[e])
                here[h].append(send(block, block, s_f.at[h, d, e - 1], r_f.at[h, d, e - 1], sibling))

    def blocks_last(h):
        for d in order:
            relay[h, d].wait_recv()
            block = kvs[h].at[lax.rem(x + 2, 4) * 8 + k * 4 + lax.rem(y + 4 - d, 4)]
            here[h].append(send(block, block, s_f.at[h, d, 3], r_f.at[h, d, 3], sibling))

    def blocks_here(h):
        for copy in here[h]:
            copy.wait()

    lane = lax.broadcasted_iota(jnp.int32, (128, 128), 1)
    left = lane < 64

    def sort(h):
        def step(j, carry):
            one = kvs[h][2 * j].astype(F32)
            two = pltpu.roll(kvs[h][2 * j + 1].astype(F32), 64, 1)
            kt[:, pl.ds(pl.multiple_of(j * 128, 128), 128)] = jnp.where(left, one, two).astype(BF)
            kt[:, pl.ds(pl.multiple_of((16 + j) * 128, 128), 128)] = jnp.where(left, two, one).astype(BF)
            return carry

        lax.fori_loop(0, 16, step, 0)
        dkv[...] = jnp.zeros_like(dkv)
        for g in range(2):
            one = qd[2 * g, h].astype(F32)
            two = pltpu.roll(qd[2 * g + 1, h].astype(F32), 64, 1)
            cols = slice(128 * g, 128 * g + 128)
            qdt[0, :, cols] = jnp.where(left, one, two)
            qdt[1, :, cols] = jnp.where(left, two, one)

    def unsort(h):
        def step(j, carry):
            low = dkv[:, pl.ds(pl.multiple_of(j * 128, 128), 128)]
            high = dkv[:, pl.ds(pl.multiple_of((16 + j) * 128, 128), 128)]
            dpart[h, 2 * j] = jnp.where(left, low, high).astype(BF)
            dpart[h, 2 * j + 1] = pltpu.roll(jnp.where(left, high, low), 64, 1).astype(BF)
            return carry

        lax.fori_loop(0, 16, step, 0)
        for g in range(2):
            cols = slice(128 * g, 128 * g + 128)
            low, high = oqt[0, :, cols], oqt[1, :, cols]
            oq[h, 2 * g] = jnp.where(left, low, high).astype(BF)
            oq[h, 2 * g + 1] = pltpu.roll(jnp.where(left, high, low), 64, 1).astype(BF)

    keys, values = slice(0, HD), slice(HD, 2 * HD)

    def one_tile(tile, between):
        q_t = qdt[tile, keys, :] * 0.125
        d_t = qdt[tile, values, :]
        q_n, d_n = q_t.T.astype(BF), d_t.T.astype(BF)
        q_t, d_t = q_t.astype(BF), d_t.astype(BF)
        first_key, last_key = s_q[tile], t_q[tile]
        top = jnp.full((256, 128), -1e30, F32)
        total = jnp.zeros((256, 128), F32)
        inner = jnp.zeros((256, 128), F32)
        for i in range(tile + 1):
            at = slice(i * CHUNK, i * CHUNK + CHUNK)
            s = dot(q_n, kt[keys, at])
            key = t_k[:, at]
            s = jnp.where((key >= first_key) & (key <= last_key), s, -1e30)
            s_buf[:, at] = s
            dp = dot(d_n, kt[values, at])
            p_buf[:, at] = dp
            new = top
            for n in range(CHUNK // 128):
                new = jnp.maximum(new, s[:, 128 * n : 128 * n + 128])
            scale = jnp.exp(top - new)
            total, inner, top = total * scale, inner * scale, new
            for n in range(CHUNK // 128):
                e = jnp.exp(s[:, 128 * n : 128 * n + 128] - new)
                total = total + e
                inner = inner + e * dp[:, 128 * n : 128 * n + 128]
        most = jnp.max(top, axis=1, keepdims=True)
        scale = jnp.exp(top - most)
        over = 1.0 / jnp.sum(total * scale, axis=1, keepdims=True)
        inner = jnp.sum(inner * scale, axis=1, keepdims=True) * over
        between()
        out_t = jnp.zeros((HD, 256), F32)
        dq_t = jnp.zeros((HD, 256), F32)
        for i in range(tile + 1):
            at = slice(i * CHUNK, i * CHUNK + CHUNK)
            p = jnp.exp(s_buf[:, at] - most) * over
            pb = p.astype(BF)
            ds = (p * (p_buf[:, at] - inner)).astype(BF)
            out_t = out_t + dot_nt(kt[values, at], pb)
            dq_t = dq_t + dot_nt(kt[keys, at], ds)
            dkv[values, at] += dot(d_t, pb)
            dkv[keys, at] += dot(q_t, ds)
        oqt[tile, keys, :] = out_t
        oqt[tile, values, :] = dq_t * 0.125

    near, beyond = {}, {}

    def grads_out(h):
        for e in (1, 3, 2, 0):
            xp = lax.rem(x + e, 4)
            near[h, e] = send(
                dpart.at[h, pl.ds(xp * 8 + (1 - k) * 4, 4)], got.at[h, xp],
                s_n.at[h, e], r_n.at[h, e], sibling,
            )
        for d in (1, 3, 2):
            yp = lax.rem(y + d, 4)
            tail.append(
                send(
                    oq.at[h, yp], out.at[y, h, pl.ds(128, 128)],
                    s_o.at[h, d - 1], r_o.at[h, d - 1], y_peer[d],
                )
            )
        out[y, h, 128:] = oq[h, y]

    def grads_on(h):
        for e in (1, 3, 2, 0):
            xp = lax.rem(x + e, 4)
            near[h, e].wait_recv()
            own = dpart[h, pl.ds(xp * 8 + k * 4, 4)]
            part[h, xp] = (own.astype(F32) + got[h, xp].astype(F32)).astype(BF)
            if e:
                beyond[h, e] = send(
                    part.at[h, xp], far.at[h, e - 1], s_a.at[h, e - 1], r_a.at[h, e - 1], x_peer[e]
                )

    def grads_last(h):
        for e in (1, 3, 2):
            beyond[h, e].wait_recv()
        for d in (1, 3, 2, 0):
            yp = lax.rem(y + d, 4)
            total = part[h, x, yp].astype(F32)
            for e in range(3):
                total = total + far[h, e, yp].astype(F32)
            if d:
                ready[h, yp] = total.astype(BF)
                tail.append(
                    send(
                        ready.at[h, yp], out.at[y, h, pl.ds(0, 128)],
                        s_b.at[h, d - 1], r_b.at[h, d - 1], y_peer[d],
                    )
                )
            else:
                out[y, h, 0:128] = total.astype(BF)

    def nothing():
        pass

    for h in range(NH):
        blocks_out(h)
    blocks_on(0)
    blocks_last(0)
    for d in (1, 3, 2):
        zp = lax.rem(z + d, 4)
        tail.append(send(zpart.at[zp], z_all.at[z], s_z.at[d - 1], r_z.at[d - 1], z_peer[d]))
    blocks_here(0)

    def later_keys():
        blocks_on(1)
        blocks_on(2)

    def last_keys():
        blocks_last(1)
        blocks_last(2)

    for h in range(NH):
        sort(h)
        one_tile(0, later_keys if h == 0 else functools.partial(grads_on, h - 1))
        one_tile(1, last_keys if h == 0 else functools.partial(grads_last, h - 1))
        unsort(h)
        grads_out(h)
        if h < NH - 1:
            blocks_here(h + 1)
    grads_on(NH - 1)
    grads_last(NH - 1)
    for copy in tail:
        copy.wait()
    for group in (first, across, relay, near, beyond):
        for copy in group.values():
            copy.wait_send()


def attend(qkvd, t_k, t_q, s_q, zpart):
    square = (128, 128)
    return pl.pallas_call(
        attend_kernel,
        out_shape=(
            jax.ShapeDtypeStruct(qkvd.shape, BF),
            jax.ShapeDtypeStruct(zpart.shape, BF),
        ),
        in_specs=vmem(5),
        out_specs=tuple(vmem(2)),
        scratch_shapes=[
            pltpu.VMEM((32,) + square, BF),
            pltpu.VMEM((32,) + square, BF),
            pltpu.VMEM((32,) + square, BF),
            pltpu.VMEM((4, NH) + square, BF),
            pltpu.VMEM((128, 4096), BF),
            pltpu.VMEM((128, 4096), F32),
            pltpu.VMEM((2, 128, 256), F32),
            pltpu.VMEM((2, 128, 256), F32),
            pltpu.VMEM((256, 4096), F32),
            pltpu.VMEM((256, 4096), F32),
            pltpu.VMEM((NH, 32) + square, BF),
            pltpu.VMEM((NH, 4) + square, BF),
            pltpu.VMEM((NH, 4, 4) + square, BF),
            pltpu.VMEM((NH, 4, 4) + square, BF),
            pltpu.VMEM((NH, 3, 4) + square, BF),
            pltpu.VMEM((NH, 4) + square, BF),
            dma(3, 3), dma(3, 3), dma(3), dma(3), dma(3, 4, 3), dma(3, 4, 3), dma(3, 4), dma(3, 4),
            dma(3, 4, 4), dma(3, 4, 4), dma(3, 4), dma(3, 4), dma(3, 3), dma(3, 3), dma(3, 3),
            dma(3, 3), dma(3, 3), dma(3, 3), dma(3), dma(3),
        ],
        compiler_params=params(1),
    )(qkvd, t_k, t_q, s_q, zpart)


def sum_kernel(
    pack, zpart, small, full, z_all, small_all,
    got, one, far_a, two, far_b, three, last, s1, s2, s3, s4,
    sz, rz, sc, rc, sa, ra, sb, rb, st, rt, gb, hb, ga, ha, gc, hc, sm, rm,
):
    z = lax.axis_index("shard")
    c, y, x, k = spots()
    sibling = {"ctx": c + 1 - 2 * k}
    z_peer = [{"shard": lax.rem(z + d, 4)} for d in range(4)]
    a = x + k * (y - x)
    b = y + k * (x - y)
    a_peer, b_peer = [], []
    for d in range(4):
        ax, by = lax.rem(a + d, 4), lax.rem(b + d, 4)
        a_peer.append({"ctx": place(b + k * (ax - b), ax + k * (b - ax), k)})
        b_peer.append({"ctx": place(by + k * (a - by), a + k * (by - a), k)})
    greet(a_peer[1:] + b_peer[1:] + z_peer[1:] + [sibling])
    near = {}
    for d in (1, 3, 2, 0):
        ap = lax.rem(b + d, 4)
        near[d] = send(pack.at[1 - k, ap], got.at[ap], sc.at[d], rc.at[d], sibling)
    tail = [send(small, s1, sm.at[0], rm.at[0], sibling)]
    for d in (1, 3, 2):
        zp = lax.rem(z + d, 4)
        tail.append(send(zpart.at[zp], z_all.at[z], sz.at[d - 1], rz.at[d - 1], z_peer[d]))
    z_all[z] = zpart[z]
    across = {}
    for d in (1, 3, 2, 0):
        ap = lax.rem(a + d, 4)
        near[d].wait_recv()
        for n in range(4):
            both = pack[k, ap, n].astype(F32) + got[ap, n].astype(F32)
            one[ap, n] = both.astype(BF)
        if d:
            across[d] = send(one.at[ap], far_a.at[d - 1], sa.at[d - 1], ra.at[d - 1], a_peer[d])
    tail[0].wait()
    s2[0] = small[...] + s1[...]
    small_a = [send(s2.at[0], s2.at[d], sm.at[d], rm.at[d], a_peer[d]) for d in (1, 2, 3)]
    for d in (1, 3, 2):
        across[d].wait_recv()
    beyond = {}
    for d in (1, 3, 2, 0):
        bp = lax.rem(b + d, 4)
        total = one[a, bp].astype(F32)
        for n in range(3):
            total = total + far_a[n, bp].astype(F32)
        two[bp] = total.astype(BF)
        if d:
            beyond[d] = send(two.at[bp], far_b.at[d - 1], sb.at[d - 1], rb.at[d - 1], b_peer[d])
    for copy in small_a:
        copy.wait()
    s3[0] = (s2[0] + s2[1]) + (s2[2] + s2[3])
    small_b = [send(s3.at[0], s3.at[d], sm.at[3 + d], rm.at[3 + d], b_peer[d]) for d in (1, 2, 3)]
    for d in (1, 3, 2):
        beyond[d].wait_recv()
    total = two[b].astype(F32)
    for n in range(3):
        total = total + far_b[n].astype(F32)
    three[...] = total.astype(BF)
    turned = []
    for d in (1, 3, 2):
        zp = lax.rem(z + d, 4)
        turned.append(
            send(
                three.at[pl.ds(2 * zp, 2)], last.at[pl.ds(2 * z, 2)],
                st.at[d - 1], rt.at[d - 1], z_peer[d],
            )
        )
    last[pl.ds(2 * z, 2)] = three[pl.ds(2 * z, 2)]
    last[8:] = three[8:]
    for copy in small_b:
        copy.wait()
    s4[...] = (s3[0] + s3[1]) + (s3[2] + s3[3])
    for d in (1, 3, 2):
        tail.append(send(s4, small_all.at[z], sm.at[6 + d], rm.at[6 + d], z_peer[d]))
    small_all[z] = s4[...]
    for copy in turned:
        copy.wait()
    full[k, a, b] = last[...]
    out_b = {}
    for d in (1, 3, 2):
        out_b[d] = send(last, full.at[k, a, b], gb.at[d - 1], hb.at[d - 1], b_peer[d])
    for d in (1, 3, 2):
        out_b[d].wait()
    out_a = {}
    for d in (1, 3, 2):
        out_a[d] = send(full.at[k, a], full.at[k, a], ga.at[d - 1], ha.at[d - 1], a_peer[d])
    tail.append(send(full.at[k, a], full.at[k, a], gc.at[0], hc.at[0], sibling))
    for d in (1, 3, 2):
        out_a[d].wait_recv()
        ap = lax.rem(a + 4 - d, 4)
        tail.append(send(full.at[k, ap], full.at[k, ap], gc.at[d], hc.at[d], sibling))
    for copy in tail[1:]:
        copy.wait()
    for d in (1, 2, 3):
        out_a[d].wait_send()
        across[d].wait_send()
        beyond[d].wait_send()
    for d in range(4):
        near[d].wait_send()


def sums(pack, zpart, small):
    tiles = pack.shape[3:]
    return pl.pallas_call(
        sum_kernel,
        out_shape=(
            jax.ShapeDtypeStruct(pack.shape, BF),
            jax.ShapeDtypeStruct(zpart.shape, BF),
            jax.ShapeDtypeStruct((4,) + small.shape, F32),
        ),
        in_specs=vmem(3),
        out_specs=tuple(vmem(3)),
        scratch_shapes=[
            pltpu.VMEM((4, 4) + tiles, BF),
            pltpu.VMEM((4, 4) + tiles, BF),
            pltpu.VMEM((3, 4) + tiles, BF),
            pltpu.VMEM((4,) + tiles, BF),
            pltpu.VMEM((3,) + tiles, BF),
            pltpu.VMEM(tiles, BF),
            pltpu.VMEM(tiles, BF),
            pltpu.VMEM(small.shape, F32),
            pltpu.VMEM((4,) + small.shape, F32),
            pltpu.VMEM((4,) + small.shape, F32),
            pltpu.VMEM(small.shape, F32),
            dma(3), dma(3), dma(4), dma(4), dma(3), dma(3), dma(3), dma(3), dma(3), dma(3),
            dma(3), dma(3), dma(3), dma(3), dma(4), dma(4), dma(10), dma(10),
        ],
        compiler_params=params(3),
    )(pack, zpart, small)


def after_kernel(flips, ret, h_all, c_all, normed, wq, w_out, cs, given, zpart, pack, small, dj, mt):
    count = h_all.shape[1]
    for s in range(4):
        cosine, sine = cs[s, 0:8], -cs[s, 8:16]
        r = [swap(ret[s, h].astype(F32), flips[s]) for h in range(NH)]
        rows = [turned(r[h][3 * HD :], cosine, sine) for h in range(NH)]
        rows += [turned(r[h][0:HD], cosine, sine) for h in range(NH)]
        rows += [r[h][HD : 2 * HD] for h in range(NH)]
        dj[count * s : count * s + count] = jnp.concatenate(rows, axis=0).T.astype(BF)
        for h in range(NH):
            mt[HD * h : HD * h + HD, count * s : count * s + count] = r[h][2 * HD : 3 * HD].astype(BF)
    cot = c_all[...].reshape(4 * count, D)
    xhat, _ = normalize(h_all[...].reshape(4 * count, D).astype(F32))
    d_one = dot_nt(dj[...], wq[...].reshape(D, 3 * HC))
    branch = dot(mt[...].astype(F32).T.astype(BF), w_out[...])
    for s in range(4):
        zpart[s, 0] = branch[count * s : count * s + count].astype(BF)
        zpart[s, 1] = d_one[count * s : count * s + count].astype(BF)
    small[...] = given[...]
    small[0:1] = jnp.sum(d_one * xhat, axis=0, keepdims=True)
    small[1:2] = jnp.sum(d_one, axis=0, keepdims=True)
    small[6:7, 0 : 3 * HC] = jnp.sum(dj[...].astype(F32), axis=0, keepdims=True)
    pack[24:32] = jnp.zeros((8,) + pack.shape[1:], BF)
    g = dot_tn(normed[...], dj[...])
    for p in range(4):
        mine = g[HC * p : HC * p + HC]
        for j in range(4):
            tiles = mine[:, 128 * j : 128 * j + 128].astype(BF).reshape(6, 2, 16, 128)
            pack[6 * j : 6 * j + 6, 2 * p : 2 * p + 2] = tiles
        rest = jnp.concatenate([mine[: HC // 2, 512:], mine[HC // 2 :, 512:]], axis=1)
        pack[24:27, 2 * p : 2 * p + 2] = rest.astype(BF).reshape(3, 2, 16, 128)
    g = dot(mt[...], cot)
    for j in range(6):
        tiles = g[:, 128 * j : 128 * j + 128].astype(BF).reshape(4, 3, 16, 128)
        pack[4 * j : 4 * j + 4, 8:11] = tiles


def after(flips, ret, h_all, c_all, normed, wq, w_out, cs, given):
    count = h_all.shape[1]
    return pl.pallas_call(
        after_kernel,
        out_shape=(
            jax.ShapeDtypeStruct((4, 2, count, D), BF),
            jax.ShapeDtypeStruct((32, 11, 16, 128), BF),
            jax.ShapeDtypeStruct((8, D), F32),
        ),
        in_specs=[pl.BlockSpec(memory_space=pltpu.SMEM)] + vmem(8),
        out_specs=tuple(vmem(3)),
        scratch_shapes=[pltpu.VMEM((4 * count, 3 * HC), BF), pltpu.VMEM((HC, 4 * count), BF)],
        compiler_params=pltpu.CompilerParams(vmem_limit_bytes=LIMIT),
    )(flips, ret, h_all, c_all, normed, wq, w_out, cs, given)


def finish_kernel(
    hid, cot, z_one, z_two, s_all, full, small_all, u0, u1, u2, u3, down,
    out, grad, g_qkv, g_out, g_up, g_down, one_g, one_b, two_g, two_b, g_bqkv, g_bout, g_bup,
):
    z = lax.axis_index("shard")
    branch, d_one, d_two = 0.0, 0.0, 0.0
    for p in range(4):
        branch = branch + (z_one[p, 0].astype(F32) + z_two[p, 0].astype(F32))
        d_one = d_one + z_one[p, 1].astype(F32)
        d_two = d_two + z_two[p, 1].astype(F32)
    flat = hid[...].astype(F32)
    xhat, r = normalize(flat)
    out[...] = (flat + branch + vector(s_all, 4) + vector(s_all, 5)).astype(BF)
    g = d_one * vector(s_all, 0) + d_two * vector(s_all, 2)
    inner = jnp.mean(g * xhat, axis=-1, keepdims=True)
    grad[...] = cot[...].astype(F32) + r * (g - jnp.mean(g, axis=-1, keepdims=True) - xhat * inner)
    planes = []
    for p in range(4):
        cols = [full[6 * j : 6 * j + 6, 2 * p : 2 * p + 2].reshape(HC, 128) for j in range(4)]
        rest = full[24:27, 2 * p : 2 * p + 2].reshape(HC // 2, 128).astype(F32)
        rest = jnp.concatenate([rest[:, :64], rest[:, 64:]], axis=0)
        planes.append(jnp.concatenate([col.astype(F32) for col in cols] + [rest], axis=1))
    for t in range(3):
        g_qkv[:, D * t : D * t + D] = jnp.concatenate(
            [plane[:, HC * t : HC * t + HC] for plane in planes], axis=1
        )
    for j in range(6):
        tiles = full[4 * j : 4 * j + 4, 8:11].reshape(HC, 128)
        g_out[:, 128 * j : 128 * j + 128] = tiles.astype(F32)
    total = (small_all[0] + small_all[1]) + (small_all[2] + small_all[3])
    own = small_all[z]
    rows = jnp.concatenate([total[0:4], own[4:5]], axis=0)
    piece = jnp.zeros((5, HC), F32)
    for p in range(4):
        piece = piece + jnp.where(z == p, rows[:, HC * p : HC * p + HC], 0.0)
    for i, ref in enumerate((one_g, one_b, two_g, two_b, g_bout)):
        ref[...] = piece[i : i + 1].reshape(HC)
    pieces = []
    for i in range(3):
        piece = jnp.zeros((1, HC), F32)
        for p in range(4):
            n = 3 * p + i
            at = HC * (n // 4)
            piece = piece + jnp.where(z == p, small_all[n % 4, 6:7, at : at + HC], 0.0)
        pieces.append(piece)
    g_bqkv[...] = jnp.concatenate(pieces, axis=1).reshape(3 * HC)
    g_bup[...] = own[5:6].reshape(g_bup.shape)
    g_down[...] = down[...].astype(F32)
    width = u0.shape[1]
    for p in range(4):
        for d, ref in enumerate((u0, u1, u2, u3)):

            @pl.when(lax.rem(z + 4 - p, 4) == d)
            def _():
                g_up[:, width * p : width * p + width] = ref[...].astype(F32)


def finish(hid, cot, z_one, z_two, s_all, full, small_all, ups, down):
    return pl.pallas_call(
        finish_kernel,
        out_shape=(
            jax.ShapeDtypeStruct(hid.shape, BF),
            jax.ShapeDtypeStruct(hid.shape, F32),
            jax.ShapeDtypeStruct((HC, 3 * D), F32),
            jax.ShapeDtypeStruct((HC, D), F32),
            jax.ShapeDtypeStruct((HC, 4 * ups[0].shape[1]), F32),
            jax.ShapeDtypeStruct(down.shape, F32),
            jax.ShapeDtypeStruct((HC,), F32),
            jax.ShapeDtypeStruct((HC,), F32),
            jax.ShapeDtypeStruct((HC,), F32),
            jax.ShapeDtypeStruct((HC,), F32),
            jax.ShapeDtypeStruct((3 * HC,), F32),
            jax.ShapeDtypeStruct((HC,), F32),
            jax.ShapeDtypeStruct((down.shape[0],), F32),
        ),
        in_specs=vmem(12),
        out_specs=tuple(vmem(13)),
        compiler_params=pltpu.CompilerParams(vmem_limit_bytes=LIMIT),
    )(hid, cot, z_one, z_two, s_all, full, small_all, *ups, down)


def local(
    hidden, ln1_gain, ln1_bias, ln2_gain, ln2_bias, w_qkv, b_qkv, w_out, b_out, w_up, b_up,
    w_down, b_down, block_order, positions, cotangent,
):
    rows = hidden.shape[0]
    c, y, x, k = spots()
    vectors = (ln1_gain, ln1_bias, ln2_gain, ln2_bias, b_out, b_down, b_qkv)
    h_all, c_all, wq, wu, s_all, p_all, o_all = spread(
        hidden, cotangent, w_qkv, w_up, vectors, positions, block_order
    )

    places = p_all.reshape(4, 64, 64)
    order = o_all.reshape(4, 64)
    blocks = jnp.arange(64, dtype=jnp.int32)

    def pick(table, which):
        hit = which[..., None] == blocks
        return jnp.sum(jnp.where(hit[..., None], table, 0), axis=-2)

    mine = lax.dynamic_slice(order, (0, 2 * c), (4, 2))
    pos = pick(places[:, None], mine).reshape(4, 1, rows)
    freqs = jnp.power(10000.0, -jnp.arange(0, ROT, 2, dtype=F32) / ROT)
    angle = pos.astype(F32) * freqs[:, None]
    cs = jnp.concatenate([jnp.cos(angle), jnp.sin(angle)], axis=1)

    order_y = lax.dynamic_index_in_dim(order, y, axis=0, keepdims=False)
    places_y = lax.dynamic_index_in_dim(places, y, axis=0, keepdims=False)
    first = order_y.reshape(32, 2)[:, 0]
    low = jnp.minimum(first, 63 - first)
    low_k = low.reshape(4, 4, 2).transpose(1, 2, 0).reshape(16, 2)
    block_k = jnp.concatenate([low_k, 63 - low_k[:, ::-1]]).reshape(64, 1)
    t_k = (block_k * 64 + blocks).reshape(1, 4096)
    low_q = lax.dynamic_index_in_dim(low.reshape(4, 8), x * 2 + k, axis=1, keepdims=False)
    flips = (mine[:, 0] >= 32).astype(jnp.int32)
    block_q = jnp.stack([low_q, 63 - low_q.reshape(2, 2)[:, ::-1].reshape(4)])
    t_q = block_q[..., None] * 64 + blocks
    s_q = t_q - pick(places_y, block_q)
    zpart_two, g_up, g_down, small = feed(
        h_all, c_all, wu, w_down, s_all, b_up.astype(F32).reshape(1, -1)
    )
    z = lax.axis_index("shard")
    ups = [lax.dynamic_index_in_dim(g_up, z, keepdims=False)]
    for d in (1, 2, 3):
        goes = lax.dynamic_index_in_dim(g_up, lax.rem(z + d, 4), keepdims=False)
        ups.append(lax.ppermute(goes, "shard", [(i, (i + d) % 4) for i in range(4)]))
    qkvd, normed = project(flips, h_all, c_all, wq, s_all, cs, w_out)
    *ups, down = lax.psum((*ups, g_down), "ctx")
    returned, z_two = attend(qkvd, t_k, t_q.reshape(2, 256, 1), s_q.reshape(2, 256, 1), zpart_two)
    zpart_one, pack, small = after(flips, returned, h_all, c_all, normed, wq, w_out, cs, small)
    full, z_one, small_all = sums(pack.reshape(2, 4, 4, 11, 16, 128), zpart_one, small)
    (
        output, grad_input, grad_qkv, grad_out, grad_up, grad_down, one_g, one_b, two_g, two_b,
        grad_bqkv, grad_bout, grad_bup,
    ) = finish(
        hidden, cotangent, z_one, z_two, s_all, full.reshape(32, 11, 16, 128), small_all, ups, down
    )
    return (
        output, grad_input, one_g, one_b, two_g, two_b, grad_qkv, grad_bqkv, grad_out, grad_bout,
        grad_up, grad_bup, grad_down, grad_bout,
    )


def solution(mesh):
    tokens, vector, matrix = P(("shard", "ctx"), None), P("shard"), P("shard", None)
    return jax.shard_map(
        local,
        mesh=mesh,
        in_specs=(
            tokens, vector, vector, vector, vector, matrix, vector, matrix, vector, matrix, vector,
            matrix, vector, matrix, matrix, tokens,
        ),
        out_specs=(
            tokens, tokens, vector, vector, vector, vector, matrix, vector, matrix, vector, matrix,
            vector, matrix, vector,
        ),
        check_vma=False,
    )
```

time: 246 us -> 231 us (0.939)
  waiting for transfers between devices: 0.03 us -> 13.8 us
  Pallas kernels: 202 us -> 189 us
  local copies, waits for them, and re-layouts: 19.7 us -> 8.38 us
  other arithmetic: 9.08 us -> 3.05 us
    pallas_call x4 -> x2, Pallas kernels: 107 us -> 92.6 us  [the longest x1 88.3 us: attend(): pl.pallas_call(attend_kernel, out_shape=(jax.ShapeDtypeStruct(qkvd.shape,...]
    ppermute x0 -> x3, waiting for transfers between devices: none -> 13.8 us  [local(): lax.ppermute(goes, 'shard', [(i, (i + d) % 4) for i in range(4)])]
    reshape x11 -> x3, local copies, waits for them, and re-layouts: 10.2 us -> 0.25 us  [the longest x2 0.16 us: local(): low_k = low.reshape(4, 4, 2).transpose(1, 2, 0).reshape(16, 2)]
    slice x5 -> x0, local copies, waits for them, and re-layouts: 4.42 us -> none  [the longest x1 1.46 us: local(): vecs[4]]
    convert_element_type x4 -> x1, other arithmetic: 4.61 us -> 0.51 us  [local(): flips = (mine[:, 0] >= 32).astype(jnp.int32)]
    pallas_call x1, Pallas kernels: 4.93 us -> 7.71 us  [finish(): pl.pallas_call(finish_kernel, out_shape=(jax.ShapeDtypeStruct(hid.shape,...]
  transfers between devices with their start and end apart: 1 -> 4, of which waited for: 0 -> 3; matrix products, arithmetic and copies ran while one was open for 3% -> 3% of each run, Pallas kernels for 52% -> 60%
where the time goes in v2:
time: 231 us
  Pallas kernels  189 us (82%)
  between operations  14.2 us (6%)
  waiting for transfers between devices  13.8 us (6%)
  local copies, waits for them, and re-layouts  8.38 us (4%)
  other arithmetic  3.05 us (1%)
    pallas_call x1, Pallas kernels, attend(): pl.pallas_call(attend_kernel, out_shape=(jax.ShapeDtypeStruct(qkvd.shape,...  88.3 us
    pallas_call x1, Pallas kernels, sums(): pl.pallas_call(sum_kernel, out_shape=(jax.ShapeDtypeStruct(pack.shape, BF...  39.7 us
    pallas_call x1, Pallas kernels, spread(): pl.pallas_call(spread_kernel, out_shape=(jax.ShapeDtypeStruct((4, rows, D...  36 us
    ppermute x3, waiting for transfers between devices, local(): lax.ppermute(goes, 'shard', [(i, (i + d) % 4) for i in range(4)])  13.8 us
    pallas_call x1, Pallas kernels, finish(): pl.pallas_call(finish_kernel, out_shape=(jax.ShapeDtypeStruct(hid.shape,...  7.71 us
    pallas_call x1, Pallas kernels, feed(): pl.pallas_call(feed_kernel, out_shape=(jax.ShapeDtypeStruct((4, 2, count,...  7.68 us
    pallas_call x1, Pallas kernels, after(): pl.pallas_call(after_kernel, out_shape=(jax.ShapeDtypeStruct((4, 2, count...  5.79 us
  transfers between devices with their start and end apart: 4, of which 3 were waited for; matrix products, arithmetic and copies ran while one was open for 3% of the time, Pallas kernels for 60%

profile of v2, /device:TPU:1, one launch (start us, length us, event | category | flops | bytes accessed | tf_op | source)
XLA Modules:
  0.0 231.1 jit_solution(1516502447639274840)
XLA Ops:
  7.2 0.0 all-reduce.3.cloned.1.call-start
  7.2 1.3 reshape.236.b_up
  8.5 36.0 %shard_map.263 = (bf16[4,128,768]{2,1,0:T(8,128)(2,1)}, bf16[4,128,768]{2,1,0:T(8,128)(2,1)}, bf16[4,192,576]{2,1,0:T(8,128)(2,1)}, bf16[4,192,768]{2,1,0:T(8,12...) custom-call(bf16[128,768]{1,0:T(8,128)(2,1)} %hid.3, bf16[128,768]{1,0:T(8,128)(2,1)} %cot.3, ...), custom_call_target="tpu_custom_call" | custom-call | tf_op jit(solution)/shard_map/pallas_call | solution.py:151
  44.5 7.7 %shard_map.265 = (bf16[4,2,128,768]{3,2,1,0:T(8,128)(2,1)}, bf16[4,192,768]{2,1,0:T(8,128)(2,1)}, bf16[768,768]{1,0:T(8,128)(2,1)}, f32[8,768]{1,0:T(8,128)}) custom-call(bf16[4,128,768]{2,1,0:T(8,128)(2,1)} %get-tuple-element.49.h_all, bf16[4,128,768]{2,1,0:T(8,128)(2,1)} %get-tuple-element.50.c_all, bf16[4,192,768]{2,1,0:T(8,128)(2,1)} %get-tuple-element.55.wu, ...), custom_call_target="tpu_custom_call" | custom-call | tf_op jit(solution)/shard_map/pallas_call | solution.py:277
  52.2 0.0 copy-start.4
  52.2 0.0 copy-start.3
  52.2 2.1 dynamic-slice_bitcast_fusion
  54.2 1.5 collective-permute-start.2
  55.8 0.6 collective-permute-start.1
  56.4 0.0 collective-permute-start
  56.4 0.0 copy-done.4
  56.4 0.1 reshape.227
  56.5 0.1 slice_reduce_fusion
  56.7 0.1 squeeze.28
  56.7 0.1 squeeze.27
  56.9 0.0 copy-done.3
  56.9 0.2 reduce
  57.0 0.1 constant_dynamic-slice_fusion.1
  57.1 0.1 copy.54
  57.2 0.1 copy.55
  57.3 0.1 iota_compare_fusion.1
  57.4 0.2 dynamic-slice_reduce_fusion
  57.6 0.1 reshape.229
  57.7 0.1 rev.7
  57.8 0.1 sub.50
  57.9 0.1 iota_compare_fusion
  58.0 0.1 copy.56
  58.1 0.1 reshape.228
  58.2 0.1 copy.58
  58.3 0.1 add_multiply_fusion
  58.4 0.1 copy.59
  58.4 0.1 mul.55
  58.6 0.1 broadcast_in_dim.48
  58.7 0.1 iota_add_fusion
  58.8 2.9 %collective-permute-done.2 = bf16[192,768]{1,0:T(8,128)(2,1)S(1)} collective-permute-done((bf16[192,768]{1,0:T(8,128)(2,1)S(1)}, bf16[192,768]{1,0:T(8,128)(2,1)S(1)}, u32[]{:S(2)}, u32[]{:S(2)}) %collective-permute-start.2) | collective-permute-done | bytes 294944 | tf_op jit(solution)/shard_map/ppermute | solution.py:869
  61.7 0.0 copy-start
  61.7 2.4 %collective-permute-done.1 = bf16[192,768]{1,0:T(8,128)(2,1)S(1)} collective-permute-done((bf16[192,768]{1,0:T(8,128)(2,1)S(1)}, bf16[192,768]{1,0:T(8,128)(2,1)S(1)}, u32[]{:S(2)}, u32[]{:S(2)}) %collective-permute-start.1) | collective-permute-done | bytes 294944 | tf_op jit(solution)/shard_map/ppermute | solution.py:869
  64.1 0.0 copy-start.1
  64.1 8.5 %collective-permute-done = bf16[192,768]{1,0:T(8,128)(2,1)S(1)} collective-permute-done((bf16[192,768]{1,0:T(8,128)(2,1)S(1)}, bf16[192,768]{1,0:T(8,128)(2,1)S(1)}, u32[]{:S(2)}, u32[]{:S(2)}) %collective-permute-start) | collective-permute-done | bytes 294944 | tf_op jit(solution)/shard_map/ppermute | solution.py:869
  72.5 0.0 copy-start.2
  72.5 0.0 copy-done
  72.5 0.0 copy-done.1
  72.6 0.7 copy-done.2
  73.3 0.0 all-reduce.3.cloned.1.call-update
  73.3 0.1 select_reduce_fusion.1
  73.4 0.1 add.114
  73.5 0.7 add.108.t_k
  74.2 0.1 convert_element_type.20
  74.3 0.1 select_reduce_fusion
  74.5 0.2 reduce_sum.23
  74.7 0.1 add.111
  74.7 0.2 add.125
  75.0 0.1 multiply_cosine_fusion
  75.1 0.6 pad_maximum_fusion.cs
  75.7 0.5 fusion.1.flips
  76.3 4.2 %shard_map.264 = (bf16[4,3,256,128]{3,2,1,0:T(8,128)(2,1)}, bf16[512,768]{1,0:T(8,128)(2,1)}) custom-call(s32[4]{0:T(128)} %fusion.1.flips, bf16[4,128,768]{2,1,0:T(8,128)(2,1)} %get-tuple-element.49.h_all, bf16[4,128,768]{2,1,0:T(8,128)(2,1)} %get-tuple-element.50.c_all, bf16[4,192,576]{2,1,0:T(8,128)(2,1)} %get-tuple-element.51.wq, ...), custom_call_target="tpu_custom_call" | custom-call | tf_op jit(solution)/shard_map/pallas_call | solution.py:238
  80.5 1.0 fusion.3
  81.5 88.3 %shard_map.266 = (bf16[4,3,256,128]{3,2,1,0:T(8,128)(2,1)}, bf16[4,2,128,768]{3,2,1,0:T(8,128)(2,1)}) custom-call(bf16[4,3,256,128]{3,2,1,0:T(8,128)(2,1)} %get-tuple-element.54.qkvd, s32[1,4096]{1,0:T(1,128)} %add.108.t_k, s32[2,256,1]{2,1,0:T(8,128)} %get-tuple-element.88.t_q, s32[2,256,1]{2,1,0:T(8,128)} %get-tuple-element.87.s_q, ...), custom_call_target="tpu_custom_call" | custom-call | tf_op jit(solution)/shard_map/pallas_call | solution.py:526
  169.8 5.8 %shard_map.267 = (bf16[4,2,128,768]{3,2,1,0:T(8,128)(2,1)}, bf16[32,11,16,128]{3,2,1,0:T(8,128)(2,1)}, f32[8,768]{1,0:T(8,128)}) custom-call(s32[4]{0:T(128)} %fusion.1.flips, bf16[4,3,256,128]{3,2,1,0:T(8,128)(2,1)} %get-tuple-element.57.ret, bf16[4,128,768]{2,1,0:T(8,128)(2,1)} %get-tuple-element.49.h_all, bf16[4,128,768]{2,1,0:T(8,128)(2,1)} %get-tuple-element.50.c_all, ...), custom_call_target="tpu_custom_call" | custom-call | tf_op jit(solution)/shard_map/pallas_call | solution.py:730
  175.6 39.7 %shard_map.268 = (bf16[2,4,4,11,16,128]{5,4,3,2,1,0:T(8,128)(2,1)}, bf16[4,2,128,768]{3,2,1,0:T(8,128)(2,1)}, f32[4,8,768]{2,1,0:T(8,128)}) custom-call(bf16[2,4,4,11,16,128]{5,4,3,2,1,0:T(8,128)(2,1)} %bitcast.19, bf16[4,2,128,768]{3,2,1,0:T(8,128)(2,1)} %get-tuple-element.61.zpart, f32[8,768]{1,0:T(8,128)} %get-tuple-element.62.small), custom_call_target="tpu_custom_call" | custom-call | tf_op jit(solution)/shard_map/pallas_call | solution.py:663
  215.3 0.0 all-reduce.3.cloned.1.call-done
  215.3 7.7 %shard_map.269 = (bf16[128,768]{1,0:T(8,128)(2,1)}, f32[128,768]{1,0:T(8,128)}, f32[192,2304]{1,0:T(8,128)}, f32[192,768]{1,0:T(8,128)}, f32[192,3072]{1,0:T(8,1...) custom-call(bf16[128,768]{1,0:T(8,128)(2,1)} %hid.3, ...), custom_call_target="tpu_custom_call" | custom-call | tf_op jit(solution)/shard_map/pallas_call | solution.py:802
  223.0 1.2 copy.69
  (11 shorter events, 0.1 us)
Async XLA Ops:
  7.2 208.1 %all-reduce.3.cloned.1.call-start = ((), (), s32[]{:S(2)}) async-start(), calls=%async_computation | async-start | bytes 4718592 | tf_op jit(solution)/shard_map/psum | solution.py:871
  52.2 4.2 %copy-start.4 = (s32[4,1,64]{2,1,0:T(1,128)S(1)}, s32[4,1,64]{2,1,0:T(1,128)}, u32[]{:S(2)}) copy-start(s32[4,1,64]{2,1,0:T(1,128)} %get-tuple-element.48) | copy-start | bytes 3076
  52.2 4.7 %copy-start.3 = (s32[4,1,4096]{2,1,0:T(1,128)S(1)}, s32[4,1,4096]{2,1,0:T(1,128)}, u32[]{:S(2)}) copy-start(s32[4,1,4096]{2,1,0:T(1,128)} %get-tuple-element.53) | copy-start | bytes 196612
  54.2 7.4 %collective-permute-start.2 = (bf16[192,768]{1,0:T(8,128)(2,1)S(1)}, bf16[192,768]{1,0:T(8,128)(2,1)S(1)}, u32[]{:S(2)}, u32[]{:S(2)}) collective-permute-start(bf16[192,768]{1,0:T(8,128)(2,1)S(1)} %get-tuple-element.89), channel_id=1, source_target_pairs={{0,3},{1,0},{2,1},{3,2},{4,7},{5,4},{6,5},{7,6},{8,11},{9,8},{10,9... | collective-permute-start | bytes 884744 | tf_op jit(solution)/shard_map/ppermute | solution.py:869
  55.8 8.3 %collective-permute-start.1 = (bf16[192,768]{1,0:T(8,128)(2,1)S(1)}, bf16[192,768]{1,0:T(8,128)(2,1)S(1)}, u32[]{:S(2)}, u32[]{:S(2)}) collective-permute-start(bf16[192,768]{1,0:T(8,128)(2,1)S(1)} %get-tuple-element.90), channel_id=1, source_target_pairs={{0,2},{1,3},{2,0},{3,1},{4,6},{5,7},{6,4},{7,5},{8,10},{9,11},{10,... | collective-permute-start | bytes 884744 | tf_op jit(solution)/shard_map/ppermute | solution.py:869
  56.4 16.1 %collective-permute-start = (bf16[192,768]{1,0:T(8,128)(2,1)S(1)}, bf16[192,768]{1,0:T(8,128)(2,1)S(1)}, u32[]{:S(2)}, u32[]{:S(2)}) collective-permute-start(bf16[192,768]{1,0:T(8,128)(2,1)S(1)} %get-tuple-element.91), channel_id=1, source_target_pairs={{0,1},{1,2},{2,3},{3,0},{4,5},{5,6},{6,7},{7,4},{8,9},{9,10},{10,1... | collective-permute-start | bytes 884744 | tf_op jit(solution)/shard_map/ppermute | solution.py:869
  61.7 10.9 %copy-start = (bf16[192,768]{1,0:T(8,128)(2,1)}, bf16[192,768]{1,0:T(8,128)(2,1)S(1)}, u32[]{:S(2)}) copy-start(bf16[192,768]{1,0:T(8,128)(2,1)S(1)} %collective-permute-done.2) | copy-start | bytes 884740
  64.1 8.5 %copy-start.1 = (bf16[192,768]{1,0:T(8,128)(2,1)}, bf16[192,768]{1,0:T(8,128)(2,1)S(1)}, u32[]{:S(2)}) copy-start(bf16[192,768]{1,0:T(8,128)(2,1)S(1)} %collective-permute-done.1) | copy-start | bytes 884740
  72.5 0.7 copy-start.2
Sparse Core Ops, SparseCore 0:
  73.4 113.3 all-reduce.2

commit v3 on v2

--- a/solution.py
+++ b/solution.py
@@ -32,6 +32,17 @@
 
 def place(y, x, k):
     return y * 8 + x * 2 + k
+
+
+def plane(x, y, k):
+    a = x + k * (y - x)
+    b = y + k * (x - y)
+    a_peer, b_peer = [], []
+    for d in range(4):
+        ax, by = lax.rem(a + d, 4), lax.rem(b + d, 4)
+        a_peer.append({"ctx": place(b + k * (ax - b), ax + k * (b - ax), k)})
+        b_peer.append({"ctx": place(by + k * (a - by), a + k * (by - a), k)})
+    return a, b, a_peer, b_peer
 
 
 def send(src, dst, send_sem, recv_sem, where):
@@ -204,10 +215,13 @@
     )
 
 
-def project_kernel(flips, h_all, c_all, wq, s_all, cs, w_out, qkvd, normed):
+def prepare_kernel(
+    flips, h_all, c_all, wq, wu, s_all, cs, w_out, w_down, b_up, qkvd, normed, zpart, pack, small
+):
     z = lax.axis_index("shard")
     count = h_all.shape[1]
     xhat, _ = normalize(h_all[...].reshape(4 * count, D).astype(F32))
+    cot = c_all[...].reshape(4 * count, D)
     n1 = (xhat * vector(s_all, 0) + vector(s_all, 1)).astype(BF)
     normed[...] = n1
     bias = []
@@ -218,7 +232,7 @@
             piece = piece + jnp.where(z == p, s_all[n // 3, 6 + n % 3 : 7 + n % 3], 0.0)
         bias.append(piece)
     joined = dot(n1, wq[...].reshape(D, 3 * HC)) + jnp.concatenate(bias, axis=1)
-    d_mixed = dot_nt(w_out[...], c_all[...].reshape(4 * count, D))
+    d_mixed = dot_nt(w_out[...], cot)
     for s in range(4):
         jt = joined[count * s : count * s + count].T
         cosine, sine = cs[s, 0:8], cs[s, 8:16]
@@ -232,36 +246,27 @@
             ]
             qkvd[s, h] = swap(jnp.concatenate(rows, axis=0), flips[s]).astype(BF)
 
-
-def project(flips, h_all, c_all, wq, s_all, cs, w_out):
-    count = h_all.shape[1]
-    return pl.pallas_call(
-        project_kernel,
-        out_shape=(
-            jax.ShapeDtypeStruct((4, NH, 4 * HD, count), BF),
-            jax.ShapeDtypeStruct((4 * count, D), BF),
-        ),
-        in_specs=[pl.BlockSpec(memory_space=pltpu.SMEM)] + vmem(6),
-        out_specs=tuple(vmem(2)),
-        compiler_params=pltpu.CompilerParams(vmem_limit_bytes=LIMIT),
-    )(flips, h_all, c_all, wq, s_all, cs, w_out)
-
-
-def feed_kernel(h_all, c_all, wu, w_down, s_all, b_up, zpart, g_up, g_down, small):
-    count = h_all.shape[1]
-    xhat, _ = normalize(h_all[...].reshape(4 * count, D).astype(F32))
     n2 = (xhat * vector(s_all, 2) + vector(s_all, 3)).astype(BF)
     up = wu[...].reshape(D, wu.shape[2])
-    cot = c_all[...].reshape(4 * count, D)
-    hidden = dot(n2, up) + b_up[...]
+    hidden = dot(n2, up) + b_up[...].astype(F32).reshape(1, b_up.shape[0])
     rise = 0.5 * (1.0 + lax.erf(hidden * (1.0 / math.sqrt(2.0))))
     slope = rise + hidden * jnp.exp(-0.5 * hidden * hidden) * (1.0 / math.sqrt(2.0 * math.pi))
     active = (hidden * rise).astype(BF)
-    d_up_f = (dot_nt(cot, w_down[...]) * slope).astype(BF)
-    g_down[...] = dot_tn(active, cot).astype(BF)
-    g_up[...] = dot_tn(n2, d_up_f).astype(BF).reshape(g_up.shape)
+    d_up = (dot_nt(cot, w_down[...]) * slope).astype(BF)
+    g_down = dot_tn(active, cot).astype(BF)
+    for half in range(2):
+        for i in range(3):
+            at = 384 * half + 128 * i
+            tiles = g_down[:, at : at + 128].reshape(16, 3, 16, 128)
+            pack[:, half, 12 + 3 * i : 15 + 3 * i] = tiles
+    g_up = dot_tn(n2, d_up).astype(BF)
+    pack[12:16, :, 0:12] = jnp.zeros((4, 2, 12, 16, 128), BF)
+    for p in range(4):
+        for j in range(6):
+            tiles = g_up[HC * p : HC * p + HC, 128 * j : 128 * j + 128].reshape(2, 2, 3, 16, 128)
+            pack[2 * j : 2 * j + 2, :, 3 * p : 3 * p + 3] = tiles
     branch = dot(active, w_down[...]).astype(BF)
-    d_two = dot_nt(d_up_f, up)
+    d_two = dot_nt(d_up, up)
     for s in range(4):
         zpart[s, 0] = branch[count * s : count * s + count]
         zpart[s, 1] = d_two[count * s : count * s + count].astype(BF)
@@ -269,107 +274,169 @@
     small[2:3] = jnp.sum(d_two * xhat, axis=0, keepdims=True)
     small[3:4] = jnp.sum(d_two, axis=0, keepdims=True)
     small[4:5] = jnp.sum(cot.astype(F32), axis=0, keepdims=True)
-    small[5:6] = jnp.sum(d_up_f.astype(F32), axis=0, keepdims=True)
-
-
-def feed(h_all, c_all, wu, w_down, s_all, b_up):
+    small[5:6] = jnp.sum(d_up.astype(F32), axis=0, keepdims=True)
+
+
+def prepare(flips, h_all, c_all, wq, wu, s_all, cs, w_out, w_down, b_up):
     count = h_all.shape[1]
     return pl.pallas_call(
-        feed_kernel,
+        prepare_kernel,
         out_shape=(
+            jax.ShapeDtypeStruct((4, NH, 4 * HD, count), BF),
+            jax.ShapeDtypeStruct((4 * count, D), BF),
             jax.ShapeDtypeStruct((4, 2, count, D), BF),
-            jax.ShapeDtypeStruct(wu.shape, BF),
-            jax.ShapeDtypeStruct(w_down.shape, BF),
+            jax.ShapeDtypeStruct((16, 2, 21, 16, 128), BF),
             jax.ShapeDtypeStruct((8, D), F32),
         ),
-        in_specs=vmem(6),
-        out_specs=tuple(vmem(4)),
+        in_specs=[pl.BlockSpec(memory_space=pltpu.SMEM)] + vmem(9),
+        out_specs=tuple(vmem(5)),
         compiler_params=pltpu.CompilerParams(vmem_limit_bytes=LIMIT),
-    )(h_all, c_all, wu, w_down, s_all, b_up)
+    )(flips, h_all, c_all, wq, wu, s_all, cs, w_out, w_down, b_up)
 
 
 def attend_kernel(
-    qkvd, t_k, t_q, s_q, zpart, out, z_all,
-    kv0, kv1, kv2, qd, kt, dkv, qdt, oqt, s_buf, p_buf, dpart, oq, got, part, far, ready,
-    s_y, r_y, s_q1, r_q1, s_x, r_x, s_r, r_r, s_f, r_f, s_n, r_n, s_a, r_a, s_b, r_b, s_o, r_o, s_z, r_z,
+    qkvd, t_k, t_q, s_q, zpart, pack, out, z_all, full,
+    in_a, in_b, kv_a, kv_b, kt, dkv, qdt, oqt, s_buf, p_buf, dpart, got, part, far, ready,
+    w_got, w_one, w_far, w_two, w_beyond, w_three, w_last,
+    s_y, r_y, s_x, r_x, s_r, r_r, s_f, r_f, s_n, r_n, s_a, r_a, s_b, r_b, s_z, r_z,
+    w_sc, w_rc, w_sa, w_ra, w_sb, w_rb, w_sz, w_rz, w_gb, w_hb, w_ga, w_ha, w_gc, w_hc,
 ):
     z = lax.axis_index("shard")
     c, y, x, k = spots()
-    kvs = (kv0, kv1, kv2)
     base = x * 8 + k * 4
     sibling = {"ctx": c + 1 - 2 * k}
     y_peer = [{"ctx": place(lax.rem(y + d, 4), x, k)} for d in range(4)]
     x_peer = [{"ctx": place(y, lax.rem(x + d, 4), k)} for d in range(4)]
     z_peer = [{"shard": lax.rem(z + d, 4)} for d in range(4)]
+    a, b, a_peer, b_peer = plane(x, y, k)
     greet(y_peer[1:] + x_peer[1:] + z_peer[1:] + [sibling])
-    tail, first, across, relay, here = [], {}, {}, {}, {0: [], 1: [], 2: []}
-    order = (0, 1, 3, 2)
-    for h in range(NH):
-        for d in order[1:]:
-            yp = lax.rem(y + d, 4)
-            first[h, d] = send(
-                qkvd.at[yp, h, pl.ds(0, 128)], kvs[h].at[base + y],
-                s_y.at[h, d - 1], r_y.at[h, d - 1], y_peer[d],
+    tail, first, across, relay, here = [], {}, {}, {}, ([], [])
+    ins, kvs = (in_a, in_b), (kv_a, kv_b)
+    heads = (slice(0, 1), slice(1, NH))
+    for g in range(2):
+        for d in (1, 3, 2):
+            src = qkvd.at[lax.rem(y + d, 4), pl.ds(g, 1 + g)]
+            first[g, d] = send(src, ins[g].at[y], s_y.at[g, d - 1], r_y.at[g, d - 1], y_peer[d])
+        ins[g][y] = qkvd[y, heads[g]]
+
+    def blocks_out(g):
+        for d in (1, 3, 2):
+            first[g, d].wait_recv()
+        kvs[g][pl.ds(base, 4)] = ins[g][:, :, 0:128]
+        block = kvs[g].at[pl.ds(base, 4)]
+        for e in (1, 3):
+            across[g, e] = send(block, block, s_x.at[g, e], r_x.at[g, e], x_peer[e])
+        here[g].append(send(block, block, s_f.at[g, 0], r_f.at[g, 0], sibling))
+
+    def blocks_on(g):
+        for e in (1, 3):
+            across[g, e].wait_recv()
+            slot = lax.rem(x + 4 - e, 4) * 8 + k * 4
+            part_of = kvs[g].at[pl.ds(slot + e - 1, 2)]
+            relay[g, e] = send(part_of, part_of, s_r.at[g, e], r_r.at[g, e], x_peer[e])
+            block = kvs[g].at[pl.ds(slot, 4)]
+            here[g].append(send(block, block, s_f.at[g, e], r_f.at[g, e], sibling))
+
+    def blocks_last(g):
+        for e in (1, 3):
+            relay[g, e].wait_recv()
+        block = kvs[g].at[pl.ds(lax.rem(x + 2, 4) * 8 + k * 4, 4)]
+        here[g].append(send(block, block, s_f.at[g, 2], r_f.at[g, 2], sibling))
+
+    def blocks_here(g):
+        for copy in here[g]:
+            copy.wait()
+
+    w_near, w_across, w_over, w_turn, w_out_b, w_out_a = {}, {}, {}, {}, {}, {}
+
+    def w_core():
+        for d in (1, 3, 2, 0):
+            ap = lax.rem(b + d, 4)
+            w_near[d] = send(pack.at[1 - k, ap], w_got.at[ap], w_sc.at[d], w_rc.at[d], sibling)
+
+    def w_sum_core():
+        for d in (1, 3, 2, 0):
+            ap = lax.rem(a + d, 4)
+            w_near[d].wait_recv()
+            w_one[ap] = (pack[k, ap].astype(F32) + w_got[ap].astype(F32)).astype(BF)
+            if d:
+                w_across[d] = send(
+                    w_one.at[ap], w_far.at[d - 1], w_sa.at[d - 1], w_ra.at[d - 1], a_peer[d]
+                )
+
+    def w_sum_a():
+        for d in (1, 3, 2):
+            w_across[d].wait_recv()
+        for d in (1, 3, 2, 0):
+            bp = lax.rem(b + d, 4)
+            total = w_one[a, bp].astype(F32)
+            for n in range(3):
+                total = total + w_far[n, bp].astype(F32)
+            w_two[bp] = total.astype(BF)
+            if d:
+                w_over[d] = send(
+                    w_two.at[bp], w_beyond.at[d - 1], w_sb.at[d - 1], w_rb.at[d - 1], b_peer[d]
+                )
+
+    def w_sum_b():
+        for d in (1, 3, 2):
+            w_over[d].wait_recv()
+        total = w_two[b].astype(F32)
+        for n in range(3):
+            total = total + w_beyond[n].astype(F32)
+        w_three[...] = total.astype(BF)
+        for d in (1, 3, 2):
+            zp = lax.rem(z + d, 4)
+            w_turn[d] = send(
+                w_three.at[pl.ds(3 * zp, 3)], w_last.at[pl.ds(3 * z, 3)],
+                w_sz.at[d - 1], w_rz.at[d - 1], z_peer[d],
             )
-            if h == 0:
-                here[0].append(
-                    send(
-                        qkvd.at[yp, :, pl.ds(128, 128)], qd.at[y],
-                        s_q1.at[d - 1], r_q1.at[d - 1], y_peer[d],
-                    )
-                )
-        kvs[h][base + y] = qkvd[y, h, 0:128]
-    qd[y] = qkvd[y, :, 128:]
-    z_all[z] = zpart[z]
-
-    def blocks_out(h):
-        for d in order:
-            if d:
-                first[h, d].wait_recv()
-            block = kvs[h].at[base + lax.rem(y + 4 - d, 4)]
-            for e in (1, 3):
-                across[h, d, e] = send(
-                    block, block, s_x.at[h, d, e - 1], r_x.at[h, d, e - 1], x_peer[e]
-                )
-            here[h].append(send(block, block, s_f.at[h, d, 1], r_f.at[h, d, 1], sibling))
-
-    def blocks_on(h):
-        for d in order:
-            ys = lax.rem(y + 4 - d, 4)
-            for e in (1, 3):
-                across[h, d, e].wait_recv()
-                block = kvs[h].at[lax.rem(x + 4 - e, 4) * 8 + k * 4 + ys]
-                if e == (1, 1, 3, 3)[d]:
-                    relay[h, d] = send(block, block, s_r.at[h, d], r_r.at[h, d], x_peer[e])
-                here[h].append(send(block, block, s_f.at[h, d, e - 1], r_f.at[h, d, e - 1], sibling))
-
-    def blocks_last(h):
-        for d in order:
-            relay[h, d].wait_recv()
-            block = kvs[h].at[lax.rem(x + 2, 4) * 8 + k * 4 + lax.rem(y + 4 - d, 4)]
-            here[h].append(send(block, block, s_f.at[h, d, 3], r_f.at[h, d, 3], sibling))
-
-    def blocks_here(h):
-        for copy in here[h]:
-            copy.wait()
+        w_last[pl.ds(3 * z, 3)] = w_three[pl.ds(3 * z, 3)]
+        w_last[12:] = w_three[12:]
+
+    def w_back_b():
+        for d in (1, 3, 2):
+            w_turn[d].wait()
+        full[k, a, b] = w_last[...]
+        for d in (1, 3, 2):
+            w_out_b[d] = send(
+                w_last, full.at[k, a, b], w_gb.at[d - 1], w_hb.at[d - 1], b_peer[d]
+            )
+
+    def w_back_a():
+        for d in (1, 3, 2):
+            w_out_b[d].wait()
+        for d in (1, 3, 2):
+            w_out_a[d] = send(
+                full.at[k, a], full.at[k, a], w_ga.at[d - 1], w_ha.at[d - 1], a_peer[d]
+            )
+        tail.append(send(full.at[k, a], full.at[k, a], w_gc.at[0], w_hc.at[0], sibling))
+
+    def w_back_core():
+        for d in (1, 3, 2):
+            w_out_a[d].wait_recv()
+            ap = lax.rem(a + 4 - d, 4)
+            tail.append(send(full.at[k, ap], full.at[k, ap], w_gc.at[d], w_hc.at[d], sibling))
 
     lane = lax.broadcasted_iota(jnp.int32, (128, 128), 1)
     left = lane < 64
 
     def sort(h):
+        g, i = (0, 0) if h == 0 else (1, h - 1)
+
         def step(j, carry):
-            one = kvs[h][2 * j].astype(F32)
-            two = pltpu.roll(kvs[h][2 * j + 1].astype(F32), 64, 1)
+            one = kvs[g][2 * j, i].astype(F32)
+            two = pltpu.roll(kvs[g][2 * j + 1, i].astype(F32), 64, 1)
             kt[:, pl.ds(pl.multiple_of(j * 128, 128), 128)] = jnp.where(left, one, two).astype(BF)
             kt[:, pl.ds(pl.multiple_of((16 + j) * 128, 128), 128)] = jnp.where(left, two, one).astype(BF)
             return carry
 
         lax.fori_loop(0, 16, step, 0)
         dkv[...] = jnp.zeros_like(dkv)
-        for g in range(2):
-            one = qd[2 * g, h].astype(F32)
-            two = pltpu.roll(qd[2 * g + 1, h].astype(F32), 64, 1)
-            cols = slice(128 * g, 128 * g + 128)
+        for n in range(2):
+            one = ins[g][2 * n, i, 128:].astype(F32)
+            two = pltpu.roll(ins[g][2 * n + 1, i, 128:].astype(F32), 64, 1)
+            cols = slice(128 * n, 128 * n + 128)
             qdt[0, :, cols] = jnp.where(left, one, two)
             qdt[1, :, cols] = jnp.where(left, two, one)
 
@@ -382,11 +449,11 @@
             return carry
 
         lax.fori_loop(0, 16, step, 0)
-        for g in range(2):
-            cols = slice(128 * g, 128 * g + 128)
+        for n in range(2):
+            cols = slice(128 * n, 128 * n + 128)
             low, high = oqt[0, :, cols], oqt[1, :, cols]
-            oq[h, 2 * g] = jnp.where(left, low, high).astype(BF)
-            oq[h, 2 * g + 1] = pltpu.roll(jnp.where(left, high, low), 64, 1).astype(BF)
+            ready[h, 2 * n, 128:] = jnp.where(left, low, high).astype(BF)
+            ready[h, 2 * n + 1, 128:] = pltpu.roll(jnp.where(left, high, low), 64, 1).astype(BF)
 
     keys, values = slice(0, HD), slice(HD, 2 * HD)
 
@@ -444,15 +511,6 @@
                 dpart.at[h, pl.ds(xp * 8 + (1 - k) * 4, 4)], got.at[h, xp],
                 s_n.at[h, e], r_n.at[h, e], sibling,
             )
-        for d in (1, 3, 2):
-            yp = lax.rem(y + d, 4)
-            tail.append(
-                send(
-                    oq.at[h, yp], out.at[y, h, pl.ds(128, 128)],
-                    s_o.at[h, d - 1], r_o.at[h, d - 1], y_peer[d],
-                )
-            )
-        out[y, h, 128:] = oq[h, y]
 
     def grads_on(h):
         for e in (1, 3, 2, 0):
@@ -473,69 +531,88 @@
             total = part[h, x, yp].astype(F32)
             for e in range(3):
                 total = total + far[h, e, yp].astype(F32)
+            ready[h, yp, 0:128] = total.astype(BF)
             if d:
-                ready[h, yp] = total.astype(BF)
                 tail.append(
                     send(
-                        ready.at[h, yp], out.at[y, h, pl.ds(0, 128)],
-                        s_b.at[h, d - 1], r_b.at[h, d - 1], y_peer[d],
+                        ready.at[h, yp], out.at[y, h], s_b.at[h, d - 1], r_b.at[h, d - 1], y_peer[d]
                     )
                 )
             else:
-                out[y, h, 0:128] = total.astype(BF)
+                out[y, h] = ready[h, y]
+
+    blocks_out(0)
+    blocks_on(0)
+    blocks_out(1)
+    blocks_last(0)
+    w_core()
+    for d in (1, 3, 2):
+        zp = lax.rem(z + d, 4)
+        tail.append(send(zpart.at[zp], z_all.at[z], s_z.at[d - 1], r_z.at[d - 1], z_peer[d]))
+    z_all[z] = zpart[z]
+    blocks_here(0)
+
+    def point_0():
+        blocks_on(1)
+        w_sum_core()
+
+    def point_3():
+        w_sum_b()
+
+    def point_4():
+        grads_on(1)
+        w_back_a()
 
     def nothing():
         pass
 
-    for h in range(NH):
-        blocks_out(h)
-    blocks_on(0)
-    blocks_last(0)
-    for d in (1, 3, 2):
-        zp = lax.rem(z + d, 4)
-        tail.append(send(zpart.at[zp], z_all.at[z], s_z.at[d - 1], r_z.at[d - 1], z_peer[d]))
-    blocks_here(0)
-
-    def later_keys():
-        blocks_on(1)
-        blocks_on(2)
-
-    def last_keys():
-        blocks_last(1)
-        blocks_last(2)
-
+    points = (
+        (point_0, functools.partial(blocks_last, 1)),
+        (functools.partial(grads_on, 0), point_3),
+        (point_4, nothing),
+    )
     for h in range(NH):
         sort(h)
-        one_tile(0, later_keys if h == 0 else functools.partial(grads_on, h - 1))
-        one_tile(1, last_keys if h == 0 else functools.partial(grads_last, h - 1))
+        one_tile(0, points[h][0])
+        one_tile(1, points[h][1])
         unsort(h)
         grads_out(h)
-        if h < NH - 1:
-            blocks_here(h + 1)
-    grads_on(NH - 1)
-    grads_last(NH - 1)
+        if h == 0:
+            blocks_here(1)
+            w_sum_a()
+        if h == 1:
+            grads_last(0)
+            w_back_b()
+    grads_last(1)
+    grads_on(2)
+    w_back_core()
+    grads_last(2)
     for copy in tail:
         copy.wait()
-    for group in (first, across, relay, near, beyond):
+    for group in (
+        first, across, relay, near, beyond, w_near, w_across, w_over, w_out_a
+    ):
         for copy in group.values():
             copy.wait_send()
 
 
-def attend(qkvd, t_k, t_q, s_q, zpart):
+def attend(qkvd, t_k, t_q, s_q, zpart, pack):
     square = (128, 128)
+    tiles = pack.shape[3:]
     return pl.pallas_call(
         attend_kernel,
         out_shape=(
             jax.ShapeDtypeStruct(qkvd.shape, BF),
             jax.ShapeDtypeStruct(zpart.shape, BF),
+            jax.ShapeDtypeStruct(pack.shape, BF),
         ),
-        in_specs=vmem(5),
-        out_specs=tuple(vmem(2)),
+        in_specs=vmem(6),
+        out_specs=tuple(vmem(3)),
         scratch_shapes=[
-            pltpu.VMEM((32,) + square, BF),
-            pltpu.VMEM((32,) + square, BF),
-            pltpu.VMEM((32,) + square, BF),
-            pltpu.VMEM((4, NH) + square, BF),
+            pltpu.VMEM((4, 1, 256, 128), BF),
+            pltpu.VMEM((4, 2, 256, 128), BF),
+            pltpu.VMEM((32, 1) + square, BF),
+            pltpu.VMEM((32, 2) + square, BF),
             pltpu.VMEM((128, 4096), BF),
             pltpu.VMEM((128, 4096), F32),
             pltpu.VMEM((2, 128, 256), F32),
@@ -543,17 +620,24 @@
             pltpu.VMEM((256, 4096), F32),
             pltpu.VMEM((256, 4096), F32),
             pltpu.VMEM((NH, 32) + square, BF),
-            pltpu.VMEM((NH, 4) + square, BF),
             pltpu.VMEM((NH, 4, 4) + square, BF),
             pltpu.VMEM((NH, 4, 4) + square, BF),
             pltpu.VMEM((NH, 3, 4) + square, BF),
-            pltpu.VMEM((NH, 4) + square, BF),
-            dma(3, 3), dma(3, 3), dma(3), dma(3), dma(3, 4, 3), dma(3, 4, 3), dma(3, 4), dma(3, 4),
-            dma(3, 4, 4), dma(3, 4, 4), dma(3, 4), dma(3, 4), dma(3, 3), dma(3, 3), dma(3, 3),
-            dma(3, 3), dma(3, 3), dma(3, 3), dma(3), dma(3),
+            pltpu.VMEM((NH, 4, 256, 128), BF),
+            pltpu.VMEM((4, 4) + tiles, BF),
+            pltpu.VMEM((4, 4) + tiles, BF),
+            pltpu.VMEM((3, 4) + tiles, BF),
+            pltpu.VMEM((4,) + tiles, BF),
+            pltpu.VMEM((3,) + tiles, BF),
+            pltpu.VMEM(tiles, BF),
+            pltpu.VMEM(tiles, BF),
+            dma(2, 3), dma(2, 3), dma(2, 4), dma(2, 4), dma(2, 4), dma(2, 4), dma(2, 4), dma(2, 4),
+            dma(3, 4), dma(3, 4), dma(3, 3), dma(3, 3), dma(3, 3), dma(3, 3), dma(3), dma(3),
+            dma(4), dma(4), dma(3), dma(3), dma(3), dma(3), dma(3), dma(3),
+            dma(3), dma(3), dma(3), dma(3), dma(4), dma(4),
         ],
         compiler_params=params(1),
-    )(qkvd, t_k, t_q, s_q, zpart)
+    )(qkvd, t_k, t_q, s_q, zpart, pack)
 
 
 def sum_kernel(
@@ -565,13 +649,7 @@
     c, y, x, k = spots()
     sibling = {"ctx": c + 1 - 2 * k}
     z_peer = [{"shard": lax.rem(z + d, 4)} for d in range(4)]
-    a = x + k * (y - x)
-    b = y + k * (x - y)
-    a_peer, b_peer = [], []
-    for d in range(4):
-        ax, by = lax.rem(a + d, 4), lax.rem(b + d, 4)
-        a_peer.append({"ctx": place(b + k * (ax - b), ax + k * (b - ax), k)})
-        b_peer.append({"ctx": place(by + k * (a - by), a + k * (by - a), k)})
+    a, b, a_peer, b_peer = plane(x, y, k)
     greet(a_peer[1:] + b_peer[1:] + z_peer[1:] + [sibling])
     near = {}
     for d in (1, 3, 2, 0):
@@ -742,7 +820,7 @@
 
 
 def finish_kernel(
-    hid, cot, z_one, z_two, s_all, full, small_all, u0, u1, u2, u3, down,
+    hid, cot, z_one, z_two, s_all, full, small_all, feed,
     out, grad, g_qkv, g_out, g_up, g_down, one_g, one_b, two_g, two_b, g_bqkv, g_bout, g_bup,
 ):
     z = lax.axis_index("shard")
@@ -788,17 +866,18 @@
         pieces.append(piece)
     g_bqkv[...] = jnp.concatenate(pieces, axis=1).reshape(3 * HC)
     g_bup[...] = own[5:6].reshape(g_bup.shape)
-    g_down[...] = down[...].astype(F32)
-    width = u0.shape[1]
+    for half in range(2):
+        for i in range(3):
+            tiles = feed[:, half, 12 + 3 * i : 15 + 3 * i].reshape(D, 128)
+            at = 384 * half + 128 * i
+            g_down[:, at : at + 128] = tiles.astype(F32)
     for p in range(4):
-        for d, ref in enumerate((u0, u1, u2, u3)):
-
-            @pl.when(lax.rem(z + 4 - p, 4) == d)
-            def _():
-                g_up[:, width * p : width * p + width] = ref[...].astype(F32)
-
-
-def finish(hid, cot, z_one, z_two, s_all, full, small_all, ups, down):
+        for j in range(6):
+            tiles = feed[2 * j : 2 * j + 2, :, 3 * p : 3 * p + 3].reshape(HC, 128)
+            g_up[:, D * p + 128 * j : D * p + 128 * j + 128] = tiles.astype(F32)
+
+
+def finish(hid, cot, z_one, z_two, s_all, full, small_all, feed):
     return pl.pallas_call(
         finish_kernel,
         out_shape=(
@@ -806,20 +885,20 @@
             jax.ShapeDtypeStruct(hid.shape, F32),
             jax.ShapeDtypeStruct((HC, 3 * D), F32),
             jax.ShapeDtypeStruct((HC, D), F32),
-            jax.ShapeDtypeStruct((HC, 4 * ups[0].shape[1]), F32),
-            jax.ShapeDtypeStruct(down.shape, F32),
+            jax.ShapeDtypeStruct((HC, 4 * D), F32),
+            jax.ShapeDtypeStruct((D, D), F32),
             jax.ShapeDtypeStruct((HC,), F32),
             jax.ShapeDtypeStruct((HC,), F32),
             jax.ShapeDtypeStruct((HC,), F32),
             jax.ShapeDtypeStruct((HC,), F32),
             jax.ShapeDtypeStruct((3 * HC,), F32),
             jax.ShapeDtypeStruct((HC,), F32),
-            jax.ShapeDtypeStruct((down.shape[0],), F32),
+            jax.ShapeDtypeStruct((D,), F32),
         ),
-        in_specs=vmem(12),
+        in_specs=vmem(8),
         out_specs=tuple(vmem(13)),
         compiler_params=pltpu.CompilerParams(vmem_limit_bytes=LIMIT),
-    )(hid, cot, z_one, z_two, s_all, full, small_all, *ups, down)
+    )(hid, cot, z_one, z_two, s_all, full, small_all, feed)
 
 
 def local(
@@ -859,24 +938,21 @@
     block_q = jnp.stack([low_q, 63 - low_q.reshape(2, 2)[:, ::-1].reshape(4)])
     t_q = block_q[..., None] * 64 + blocks
     s_q = t_q - pick(places_y, block_q)
-    zpart_two, g_up, g_down, small = feed(
-        h_all, c_all, wu, w_down, s_all, b_up.astype(F32).reshape(1, -1)
+    qkvd, normed, zpart_two, feed_pack, small = prepare(
+        flips, h_all, c_all, wq, wu, s_all, cs, w_out, w_down, b_up
     )
-    z = lax.axis_index("shard")
-    ups = [lax.dynamic_index_in_dim(g_up, z, keepdims=False)]
-    for d in (1, 2, 3):
-        goes = lax.dynamic_index_in_dim(g_up, lax.rem(z + d, 4), keepdims=False)
-        ups.append(lax.ppermute(goes, "shard", [(i, (i + d) % 4) for i in range(4)]))
-    qkvd, normed = project(flips, h_all, c_all, wq, s_all, cs, w_out)
-    *ups, down = lax.psum((*ups, g_down), "ctx")
-    returned, z_two = attend(qkvd, t_k, t_q.reshape(2, 256, 1), s_q.reshape(2, 256, 1), zpart_two)
+    returned, z_two, feed = attend(
+        qkvd, t_k, t_q.reshape(2, 256, 1), s_q.reshape(2, 256, 1), zpart_two,
+        feed_pack.reshape(2, 4, 4, 21, 16, 128),
+    )
     zpart_one, pack, small = after(flips, returned, h_all, c_all, normed, wq, w_out, cs, small)
     full, z_one, small_all = sums(pack.reshape(2, 4, 4, 11, 16, 128), zpart_one, small)
     (
         output, grad_input, grad_qkv, grad_out, grad_up, grad_down, one_g, one_b, two_g, two_b,
         grad_bqkv, grad_bout, grad_bup,
     ) = finish(
-        hidden, cotangent, z_one, z_two, s_all, full.reshape(32, 11, 16, 128), small_all, ups, down
+        hidden, cotangent, z_one, z_two, s_all, full.reshape(32, 11, 16, 128), small_all,
+        feed.reshape(16, 2, 21, 16, 128),
     )
     return (
         output, grad_input, one_g, one_b, two_g, two_b, grad_qkv, grad_bqkv, grad_out, grad_bout,

time: 231 us -> 194 us (0.84)
  waiting for transfers between devices: 13.8 us -> 0 us
  between operations: 14.2 us -> 0.81 us
  Pallas kernels: 189 us -> 183 us
  local copies, waits for them, and re-layouts: 8.38 us -> 5.7 us
    ppermute x3 -> x0, waiting for transfers between devices: 13.8 us -> none  [local(): lax.ppermute(goes, 'shard', [(i, (i + d) % 4) for i in range(4)])]
    pallas_call x2 -> x1, Pallas kernels: 11.9 us -> 8.94 us  [prepare(): pl.pallas_call(prepare_kernel, out_shape=(jax.ShapeDtypeStruct((4, NH, 4...]
  transfers between devices with their start and end apart: 4 -> 0, of which waited for: 3 -> 0; matrix products, arithmetic and copies ran while one was open for 3% -> 0% of each run, Pallas kernels for 60% -> 0%
where the time goes in v3:
time: 194 us; the launch traced here: 193 us
  Pallas kernels  183 us (94%)
  local copies, waits for them, and re-layouts  5.7 us (3%)
  other arithmetic  3.84 us (2%)
    pallas_call x1, Pallas kernels, attend(): pl.pallas_call(attend_kernel, out_shape=(jax.ShapeDtypeStruct(qkvd.shape,...  87.5 us
    pallas_call x1, Pallas kernels, sums(): pl.pallas_call(sum_kernel, out_shape=(jax.ShapeDtypeStruct(pack.shape, BF...  37.5 us
    pallas_call x1, Pallas kernels, spread(): pl.pallas_call(spread_kernel, out_shape=(jax.ShapeDtypeStruct((4, rows, D...  36 us
    pallas_call x1, Pallas kernels, prepare(): pl.pallas_call(prepare_kernel, out_shape=(jax.ShapeDtypeStruct((4, NH, 4...  8.94 us
    pallas_call x1, Pallas kernels, finish(): pl.pallas_call(finish_kernel, out_shape=(jax.ShapeDtypeStruct(hid.shape,...  7.38 us
    pallas_call x1, Pallas kernels, after(): pl.pallas_call(after_kernel, out_shape=(jax.ShapeDtypeStruct((4, 2, count...  5.76 us

profile of v3, /device:TPU:1, one launch (start us, length us, event | category | flops | bytes accessed | tf_op | source)
XLA Modules:
  0.0 193.4 jit_solution(14300776890514632646)
XLA Ops:
  0.7 0.1 add.82
  0.8 36.0 %shard_map.263 = (bf16[4,128,768]{2,1,0:T(8,128)(2,1)}, bf16[4,128,768]{2,1,0:T(8,128)(2,1)}, bf16[4,192,576]{2,1,0:T(8,128)(2,1)}, bf16[4,192,768]{2,1,0:T(8,12...) custom-call(bf16[128,768]{1,0:T(8,128)(2,1)} %hid.3, bf16[128,768]{1,0:T(8,128)(2,1)} %cot.3, ...), custom_call_target="tpu_custom_call" | custom-call | tf_op jit(solution)/shard_map/pallas_call | solution.py:162
  36.8 0.7 fusion.1
  37.5 0.8 constant_dynamic-slice_fusion.1
  38.2 0.1 copy.54
  38.3 0.5 fusion.2.flips
  38.9 0.1 copy.55
  39.0 0.1 iota_compare_fusion.1
  39.0 0.1 reshape.228
  39.1 0.1 slice_reduce_fusion
  39.2 0.1 squeeze.15
  39.3 0.2 dynamic-slice_reduce_fusion
  39.5 0.1 reshape.230
  39.6 0.1 rev.7
  39.7 0.1 sub.50
  39.8 0.1 iota_compare_fusion
  39.9 0.1 add.79
  40.0 0.1 squeeze.14
  40.1 0.1 copy.56
  40.2 0.1 reshape.229
  40.3 0.1 copy.58
  40.4 0.1 add_multiply_fusion
  40.5 0.1 copy.59
  40.6 0.1 mul.55
  40.7 0.1 iota_add_fusion
  40.8 0.7 add.76.t_k
  41.5 1.0 reduce
  42.5 0.1 broadcast_in_dim.48
  42.6 0.1 select_reduce_fusion.1
  42.8 0.2 select_reduce_fusion
  42.9 0.1 convert_element_type.19
  43.0 0.1 multiply_cosine_fusion
  43.2 0.6 pad_maximum_fusion.cs
  43.8 0.2 reduce_sum.23
  44.0 0.2 add.86
  44.2 0.9 fusion.3
  45.1 8.9 %shard_map.264 = (bf16[4,3,256,128]{3,2,1,0:T(8,128)(2,1)}, bf16[512,768]{1,0:T(8,128)(2,1)}, bf16[4,2,128,768]{3,2,1,0:T(8,128)(2,1)}, bf16[16,2,21,16,128]{4,3,2,1,0:T(8,128)(2,1)}, f32[8,768]{1,0:T(8,128)}) custom-call(s32[4]{0:T(128)} %fusion.2.flips, bf16[4,128,768]{2,1,0:T(8,128)(2,1)} %get-tuple-element.49.h_all, ...), custom_call_target="tpu_custom_call" | custom-call | tf_op jit(solution)/shard_map/pallas_call | solution.py:282
  54.0 87.5 %shard_map.265 = (bf16[4,3,256,128]{3,2,1,0:T(8,128)(2,1)}, bf16[4,2,128,768]{3,2,1,0:T(8,128)(2,1)}, bf16[2,4,4,21,16,128]{5,4,3,2,1,0:T(8,128)(2,1)}) custom-call(bf16[4,3,256,128]{3,2,1,0:T(8,128)(2,1)} %get-tuple-element.55.qkvd, s32[1,4096]{1,0:T(1,128)} %add.76.t_k, s32[2,256,1]{2,1,0:T(8,128)} %get-tuple-element.83.t_q, ...), custom_call_target="tpu_custom_call" | custom-call | tf_op jit(solution)/shard_map/pallas_call | solution.py:602
  141.6 5.8 %shard_map.266 = (bf16[4,2,128,768]{3,2,1,0:T(8,128)(2,1)}, bf16[32,11,16,128]{3,2,1,0:T(8,128)(2,1)}, f32[8,768]{1,0:T(8,128)}) custom-call(s32[4]{0:T(128)} %fusion.2.flips, bf16[4,3,256,128]{3,2,1,0:T(8,128)(2,1)} %get-tuple-element.58.ret, bf16[4,128,768]{2,1,0:T(8,128)(2,1)} %get-tuple-element.49.h_all, bf16[4,128,768]{2,1,0:T(8,128)(2,1)} %get-tuple-element.50.c_all, ...), custom_call_target="tpu_custom_call" | custom-call | tf_op jit(solution)/shard_map/pallas_call | solution.py:808
  147.3 37.5 %shard_map.267 = (bf16[2,4,4,11,16,128]{5,4,3,2,1,0:T(8,128)(2,1)}, bf16[4,2,128,768]{3,2,1,0:T(8,128)(2,1)}, f32[4,8,768]{2,1,0:T(8,128)}) custom-call(bf16[2,4,4,11,16,128]{5,4,3,2,1,0:T(8,128)(2,1)} %bitcast.14, bf16[4,2,128,768]{3,2,1,0:T(8,128)(2,1)} %get-tuple-element.62.zpart, f32[8,768]{1,0:T(8,128)} %get-tuple-element.63.small), custom_call_target="tpu_custom_call" | custom-call | tf_op jit(solution)/shard_map/pallas_call | solution.py:741
  184.8 7.4 %shard_map.268 = (bf16[128,768]{1,0:T(8,128)(2,1)}, f32[128,768]{1,0:T(8,128)}, f32[192,2304]{1,0:T(8,128)}, f32[192,768]{1,0:T(8,128)}, f32[192,3072]{1,0:T(8,1...) custom-call(bf16[128,768]{1,0:T(8,128)(2,1)} %hid.3, ...), custom_call_target="tpu_custom_call" | custom-call | tf_op jit(solution)/shard_map/pallas_call | solution.py:881
  192.2 1.2 copy.64
  (10 shorter events, 0.1 us)
